TPU v7x, 256 devices: a whole 4x4x8 slice. The times are simulated.
256 devices in a mesh: section: 2 (over x_hi), dp: 8 (over x_lo, y), mp: 16 (over z, core).
Axes of the slice: x: 4 (x_hi: 2, x_lo: 2; x = x_hi * 2 + x_lo), y: 4, z: 8, core: 2. Of those that a mesh axis runs over, the one named last changes fastest.
Arguments:
- handoff: bfloat16 [2, 1024, 12288], P('section', ('mp', 'dp')), may hold values from -44 to 44
- ln_gain: float32 [2, 12288], P('section', 'dp'), may hold values from 0.1 to 1.9
- ln_bias: float32 [2, 12288], P('section', 'dp'), may hold values from -3 to 3
- w_up: bfloat16 [2, 12288, 24576], P('section', 'dp', 'mp'), may hold values from -0.0546875 to 0.0546875
- up_bias: float32 [2, 24576], P('section', 'mp'), may hold values from -3 to 3
- w_down: bfloat16 [2, 24576, 12288], P('section', 'mp', 'dp'), may hold values from -0.0390625 to 0.0390625
- down_bias: float32 [2, 12288], P('section', 'dp'), may hold values from -3 to 3
Outputs:
- layer_out: bfloat16 [2, 1024, 12288], P('section', 'mp', 'dp')
All inputs are finite; a program needn't handle non-finite values.
Results may differ from a plain program's by a relative error of at most 0.0034.
Values may be sent and summed in bfloat16 or wider, within the bound.
A program may use at most 64 MiB of HBM per device.

v0:
```python
import jax
import jax.numpy as jnp
from jax import lax
from jax.sharding import PartitionSpec as P

D = 12288


def shifted(value, axis, steps):
    count = lax.axis_size(axis)
    pairs = [(source, (source + steps) % count) for source in range(count)]
    return lax.ppermute(value, axis, pairs)


def body(handoff, ln_gain, ln_bias, w_up, up_bias, w_down, down_bias):
    finished = handoff[0]
    arrived = shifted(finished, "section", 1)
    local = lax.all_to_all(arrived, "dp", split_axis=1, concat_axis=0, tiled=True)
    x = local.astype(jnp.float32)
    total = lax.psum(jnp.sum(x, axis=1), "dp")
    mean = total / D
    centered = x - mean[:, None]
    spread = lax.psum(jnp.sum(centered * centered, axis=1), "dp")
    var = spread / D
    normed = (centered * lax.rsqrt(var + 1e-05)[:, None] * ln_gain[0] + ln_bias[0]).astype(
        jnp.bfloat16
    )
    up_block = w_up[0]
    down_block = w_down[0]
    pre = jnp.dot(
        lax.all_gather(normed, "mp", axis=0, tiled=True),
        up_block,
        preferred_element_type=jnp.float32,
    )
    summed = lax.psum(pre, "dp")
    hidden = jnp.maximum(summed + up_bias[0], 0.0).astype(jnp.bfloat16)
    mixed = lax.psum_scatter(
        jnp.dot(hidden, down_block, preferred_element_type=jnp.float32),
        "mp",
        scatter_dimension=0,
        tiled=True,
    )
    result = (x + mixed + down_bias[0]).astype(jnp.bfloat16)
    return result[None]


def solution(mesh):
    placed = (
        P("section", ("mp", "dp"), None),
        P("section", "dp"),
        P("section", "dp"),
        P("section", "dp", "mp"),
        P("section", "mp"),
        P("section", "mp", "dp"),
        P("section", "dp"),
    )
    return jax.shard_map(
        body, mesh=mesh, in_specs=placed, out_specs=P("section", "mp", "dp"), check_vma=False
    )
```

profile of v0, /device:TPU:4, one launch (start us, length us, event | category | flops | bytes accessed | tf_op | source)
XLA Modules:
  0.0 347.1 jit_solution(4434889560147417297)
XLA Ops:
  6.5 2.2 collective-permute-start
  8.8 6.2 %collective-permute-done = bf16[8,12288]{1,0:T(8,128)(2,1)} collective-permute-done((bf16[8,12288]{1,0:T(8,128)(2,1)}, bf16[8,12288]{1,0:T(8,128)(2,1)}, u32[]{:S(2)}, u32[]{:S(2)}) %collective-permute-start) | collective-permute-done | bytes 196640 | tf_op jit(solution)/shard_map/ppermute | solution.py:12
  15.0 5.1 %all-to-all-start = ((bf16[8,8,1536]{2,0,1:T(8,128)(2,1)}), bf16[8,8,1536]{2,0,1:T(8,128)(2,1)S(1)}, u32[]{:S(2)}, u32[]{:S(2)}) async-start(bf16[8,8,1536]{2,0,1:T(8,128)(2,1)} %bitcast.1), calls=%async_computation | async-start | bytes 393216 | tf_op jit(solution)/shard_map/all_to_all | solution.py:18
  20.1 0.7 reduce.2
  20.9 0.7 reduce.3
  21.6 5.5 %all-to-all-done = bf16[8,8,1536]{2,0,1:T(8,128)(2,1)S(1)} async-done(((bf16[8,8,1536]{2,0,1:T(8,128)(2,1)}), bf16[8,8,1536]{2,0,1:T(8,128)(2,1)S(1)}, u32[]{:S(2)}, u32[]{:S(2)}) %all-to-all-start) | async-done | bytes 196640 | tf_op jit(solution)/shard_map/all_to_all | solution.py:18
  27.0 0.1 fusion.6
  27.1 0.1 reduce_sum.23
  27.2 17.4 %psum.21 = f32[64]{0:T(128)S(1)} all-reduce(f32[64]{0:T(128)S(1)} %reduce_sum.23), channel_id=1, replica_groups=mesh['section'=2,'dp'=8,'mp'=16] {'dp'}, use_global_device_ids=true, to_apply=%region_1.0 | all-reduce | flops 64 | bytes 512 | tf_op jit(solution)/shard_map/psum | solution.py:20
  44.6 0.1 sub.17
  44.7 0.2 fusion.17
  44.9 0.1 reduce_sum.25
  45.0 16.5 %psum.22 = f32[64]{0:T(128)S(1)} all-reduce(f32[64]{0:T(128)S(1)} %reduce_sum.25), channel_id=1, replica_groups=mesh['section'=2,'dp'=8,'mp'=16] {'dp'}, use_global_device_ids=true, to_apply=%region_3.0 | all-reduce | flops 64 | bytes 512 | tf_op jit(solution)/shard_map/psum | solution.py:23
  61.5 0.8 fusion.13
  62.4 0.0 all-reduce.2.cloned.1.call-start
  62.4 42.3 %all-gather.2.cloned.1.call-done = bf16[1024,1536]{1,0:T(8,128)(2,1)} async-done(((bf16[64,1536]{1,0:T(8,128)(2,1)}), bf16[1024,1536]{1,0:T(8,128)(2,1)}) %all-gather.2.cloned.1.call-update) | async-done | bytes 3145744 | tf_op jit(solution)/shard_map/all_gather | solution.py:31
  104.7 9.7 %fusion.2 = f32[1024,1536]{1,0:T(8,128)} fusion(bf16[1024,1536]{1,0:T(8,128)(2,1)} %all-gather.2.cloned.1.call-done, bf16[1,1536,1536]{2,1,0:T(8,128)(2,1)} %param.10), kind=kOutput, calls=%fused_computation.3 | convolution fusion | flops 4831838208 | bytes 14155776 | tf_op jit(solution)/shard_map/dot_general | solution.py:30
  114.4 0.0 reduce-scatter.2.cloned.1.call-start
  114.4 0.6 copy-done
  115.1 147.8 %all-reduce.2.cloned.1.call-done = f32[1024,1536]{1,0:T(8,128)} async-done(((f32[1024,1536]{1,0:T(8,128)}), f32[1024,1536]{1,0:T(8,128)}) %all-reduce.2.cloned.1.call-update) | async-done | bytes 6291472 | tf_op jit(solution)/shard_map/psum | solution.py:35
  262.8 10.1 %fusion = f32[1024,1536]{1,0:T(8,128)} fusion(bf16[1,1536,1536]{2,1,0:T(8,128)(2,1)} %param.12, f32[1024,1536]{1,0:T(8,128)} %all-reduce.2.cloned.1.call-done, f32[1536]{0:T(1024)S(1)} %reduce.4), kind=kOutput, calls=%fused_computation.1 | convolution fusion | flops 4836556800 | bytes 17307648 | tf_op jit(solution)/shard_map/dot_general | solution.py:38
  273.0 0.7 copy-done.1
  273.7 65.2 %reduce-scatter.2.cloned.1.call-done = f32[64,1536]{1,0:T(8,128)} async-done(((f32[1024,1536]{1,0:T(8,128)}), f32[64,1536]{1,0:T(8,128)}) %reduce-scatter.2.cloned.1.call-update) | async-done | bytes 393232 | tf_op jit(solution)/shard_map/reduce_scatter | solution.py:37
  338.9 1.7 fusion.18
  (10 shorter events, 0.1 us)
Async XLA Ops:
  6.5 8.5 %collective-permute-start = (bf16[8,12288]{1,0:T(8,128)(2,1)}, bf16[8,12288]{1,0:T(8,128)(2,1)}, u32[]{:S(2)}, u32[]{:S(2)}) collective-permute-start(bf16[8,12288]{1,0:T(8,128)(2,1)} %bitcast.42), channel_id=1, source_target_pairs={{0,128},{128,0},{1,129},{129,1},{2,130},{130,2},{3,131},{131,3},{4... | collective-permute-start | bytes 589832 | tf_op jit(solution)/shard_map/ppermute | solution.py:12
  15.0 12.0 %all-to-all-start = ((bf16[8,8,1536]{2,0,1:T(8,128)(2,1)}), bf16[8,8,1536]{2,0,1:T(8,128)(2,1)S(1)}, u32[]{:S(2)}, u32[]{:S(2)}) async-start(bf16[8,8,1536]{2,0,1:T(8,128)(2,1)} %bitcast.1), calls=%async_computation | async-start | bytes 393216 | tf_op jit(solution)/shard_map/all_to_all | solution.py:18
  20.1 84.6 %all-gather.2.cloned.1.call-start = ((), (), s32[]{:S(2)}) async-start(), calls=%async_computation.2 | async-start | bytes 3342336 | tf_op jit(solution)/shard_map/all_gather | solution.py:31
  62.4 200.5 %all-reduce.2.cloned.1.call-start = ((), (), s32[]{:S(2)}) async-start(), calls=%async_computation.3 | async-start | bytes 12582912 | tf_op jit(solution)/shard_map/psum | solution.py:35
  114.3 0.7 copy-start
  114.4 224.5 %reduce-scatter.2.cloned.1.call-start = ((), (), s32[]{:S(2)}) async-start(), calls=%async_computation.4 | async-start | bytes 6684672 | tf_op jit(solution)/shard_map/reduce_scatter | solution.py:37
  273.0 0.7 copy-start.1
Sparse Core Ops, SparseCore 0:
  62.5 42.1 all-gather.1
  114.5 148.2 all-reduce.1
  273.1 65.7 reduce-scatter.1
where the time goes:
time: 348 us; the launch traced here: 347 us
  waiting for transfers between devices  267 us (77%)
  blocking collectives  33.9 us (10%)
  matrix products  19.8 us (6%)
  between operations  13.1 us (4%)
  starting transfers between devices  7.47 us (2%)
  other arithmetic  4.35 us (1%)
    psum x1, waiting for transfers between devices, body(): summed = lax.psum(pre, 'dp')  148 us
    reduce_scatter x1, waiting for transfers between devices, body(): lax.psum_scatter(jnp.dot(hidden, down_block, preferred_element_type=jnp.f...  65.2 us
    all_gather x1, waiting for transfers between devices, body(): lax.all_gather(normed, 'mp', axis=0, tiled=True)  42.3 us
    psum x1, blocking collectives, body(): total = lax.psum(jnp.sum(x, axis=1), 'dp')  17.4 us
    psum x1, blocking collectives, body(): spread = lax.psum(jnp.sum(centered * centered, axis=1), 'dp')  16.5 us
    dot_general x1, matrix products, body(): jnp.dot(hidden, down_block, preferred_element_type=jnp.float32)  10.1 us
    dot_general x1, matrix products, body(): jnp.dot(lax.all_gather(normed, 'mp', axis=0, tiled=True), up_block, prefe...  9.66 us
  transfers between devices with their start and end apart: 5, of which 5 were waited for; matrix products, arithmetic and copies ran while one was open for 0% of the time, Pallas kernels for 0%

commit v1 on v0

v1 whole, which is shorter than its diff:
```python
import functools

import jax
import jax.numpy as jnp
from jax import lax
from jax.experimental import pallas as pl
from jax.experimental.pallas import tpu as pltpu
from jax.sharding import PartitionSpec as P

D = 12288
W = 1536
N = 8
CA = 768
CB = W - CA
HA = CA // 2
F32 = jnp.float32
BF16 = jnp.bfloat16
MESH = pl.DeviceIdType.MESH

OFFSETS = {"s2": 1, "s3": 2, "s4": 3, "s5": 4, "s6": 5, "g2": 6}
ORDER = ("ag", "g1", "s2", "s3", "s4", "s5", "s6", "g2", "z")
AG_SLOT = {1: 1, 2: 2, 3: 3, 4: 3}
Z_SLOT = {4: 9, 3: 11, 2: 13, 1: 14, 0: 14}
SLOTS = 15

SCRATCH = dict(
    hand=((8, D), BF16),
    wup=((W, W), BF16),
    wdn=((W, W), BF16),
    gain=((1, W), F32),
    bias=((1, W), F32),
    ubias=((1, W), F32),
    dbias=((1, W), F32),
    hs=((8, 16, 896), BF16),
    hr=((8, 16, 896), BF16),
    xres=((64, W), F32),
    nrm=((N, 128, W), BF16),
    paf=((N, 128, CA), F32),
    pbf=((N, 128, CB), F32),
    pab=((N, 128, CA), BF16),
    pbb=((N, 128, CB), BF16),
    a1=((N, 64, CA), BF16),
    a2=((N, 2, 16, HA), BF16),
    a3=((N, 2, 16, CA), BF16),
    b1=((N, 2, 16, CB), BF16),
    b2=((N, 2, 32, CB), BF16),
    b3=((N, 16, CB), BF16),
    fa=((N, 2, 16, HA), BF16),
    na=((N, 2, 16, CA), BF16),
    nb=((N, 2, 32, CB), BF16),
    xb=((N, 16, CB), BF16),
    hida=((N, 128, CA), BF16),
    hidb=((N, 128, CB), BF16),
    pf=((N, 128, W), F32),
    so=((N, 64, W), BF16),
    sib=((N, 64, W), BF16),
    zs=((N, 64, W), BF16),
    zr=((N, 64, W), BF16),
)
SENDS = ("hand", "agc", "agz", "a1", "a2", "a3", "b1", "b2", "b3", "a4", "a5", "a6", "b4", "b5", "b6", "so", "zr")
RECVS = ("agc", "agz", "a1", "a2", "a3", "b1", "b2", "b3", "a4", "a5", "a6", "b4", "b5", "b6", "so", "zr")


def kernel(hand_in, gain_in, bias_in, wup_in, ubias_in, wdn_in, dbias_in, out, *refs):
    v = dict(zip(SCRATCH, refs))
    local_sem, hand_sem, send_sem, recv_sem = refs[len(SCRATCH):]
    s = lax.axis_index("section")
    d = lax.axis_index("dp")
    m = lax.axis_index("mp")
    xl, y, z, c = d // 4, d % 4, m // 2, m % 2
    y_up, y_far, y_dn = (y + 1) % 4, (y + 2) % 4, (y + 3) % 4
    z_up, z_dn = (z + 1) % N, (z + N - 1) % N

    def at(section=s, x=xl, row=y, deep=z, core=c):
        return (section, x * 4 + row, deep * 2 + core)

    sibling = at(core=1 - c)
    x_other = at(x=1 - xl)
    above, below = at(row=y_up), at(row=y_dn)
    ahead, behind = at(deep=z_up), at(deep=z_dn)

    loads = []
    for i, (src, dst) in enumerate((
        (hand_in, "hand"), (gain_in, None), (bias_in, None), (ubias_in, None), (dbias_in, None),
        (wup_in, "wup"), (wdn_in, "wdn"),
    )):
        name = ("hand", "gain", "bias", "ubias", "dbias", "wup", "wdn")[i]
        from_ref = src.at[0] if dst else src
        load = pltpu.make_async_copy(from_ref, v[name], local_sem.at[i])
        load.start()
        loads.append(load)

    barrier = pltpu.get_barrier_semaphore()
    others = [(1 - s, i, m) for i in range(8)]
    near = [sibling, x_other, above, below, ahead, behind]
    for device in others + near:
        pl.semaphore_signal(barrier, inc=1, device_id=device, device_id_type=MESH)

    def send(kind, k, src, dst, device):
        pltpu.make_async_remote_copy(
            src_ref=src,
            dst_ref=dst,
            send_sem=send_sem.at[SENDS.index(kind)],
            recv_sem=recv_sem.at[RECVS.index(kind), k],
            device_id=device,
            device_id_type=MESH,
        ).start()

    def arrived(kind, k, like):
        pltpu.make_async_copy(like, like, recv_sem.at[RECVS.index(kind), k]).wait()

    def rows(start, size):
        return pl.ds(pl.multiple_of(start, 16), size)

    loads[0].wait()
    x = v["hand"][...].astype(F32)
    mean = jnp.sum(x, axis=1, keepdims=True) / D
    centred = x - mean
    rstd = lax.rsqrt(jnp.sum(centred * centred, axis=1, keepdims=True) / D + 1e-05)
    lane = lax.broadcasted_iota(jnp.int32, (8, 128), 1)

    def parts(value):
        high = value.astype(BF16).astype(F32)
        rest = value - high
        middle = rest.astype(BF16).astype(F32)
        low = rest - middle
        return jnp.where(lane < 32, high, jnp.where(lane < 64, middle, low))

    stats = jnp.concatenate([parts(mean), parts(rstd)], axis=0).astype(BF16)
    for i in range(8):
        left = x[:, i * W:i * W + 768]
        right = x[:, i * W + 768:(i + 1) * W]
        v["hs"][i, :, :768] = jnp.concatenate([left, right], axis=0).astype(BF16)
        v["hs"][i, :, 768:] = stats
    pl.semaphore_wait(barrier, len(others) + len(near))
    for i in range(8):
        pltpu.make_async_remote_copy(
            src_ref=v["hs"].at[i],
            dst_ref=v["hr"].at[d],
            send_sem=send_sem.at[0],
            recv_sem=hand_sem,
            device_id=others[i],
            device_id_type=MESH,
        ).start()
    for load in loads[1:5]:
        load.wait()
    pltpu.make_async_copy(v["hr"], v["hr"], hand_sem).wait()

    def unpack(i):
        held = v["hr"][i].astype(F32)
        stat = held[:, 768:]
        stat = stat[:, 0:1] + stat[:, 32:33] + stat[:, 64:65]
        return jnp.concatenate([held[:8, :768], held[8:, :768]], axis=1), stat[:8], stat[8:]

    for i in range(4):
        xa, mean_a, rstd_a = unpack(2 * i)
        xb, mean_b, rstd_b = unpack(2 * i + 1)
        two = jnp.concatenate([(xa - mean_a) * rstd_a, (xb - mean_b) * rstd_b], axis=0)
        v["nrm"][z, rows(c * 64 + i * 16, 16), :] = (two * v["gain"][...] + v["bias"][...]).astype(BF16)
        v["xres"][i * 16:i * 16 + 16, :] = jnp.concatenate([xa, xb], axis=0)

    def rel(k):
        return k + jnp.where(k == 3, 1, 0) - jnp.where(k == 4, 1, 0)

    def pos(r):
        return {4: 3, 3: 4}.get(r, r)

    def block(r, first=0, size=64):
        return v["nrm"].at[(z + r) % N, rows(c * 64 + first, size)]

    def ring(r, first, size, device, there):
        send("agz", there % N, block(r, first, size), block(r, first, size), device)

    def pair(r):
        send("agc", r % N, block(r), block(r), sibling)

    pair(0)
    ring(0, 0, 64, ahead, -1)
    ring(0, 0, 64, behind, 1)

    def gather(h):
        if h == 4:
            arrived("agz", 4, v["zr"].at[0])
            pair(4)
            return
        for r, device, step in ((-h, ahead, -1), (h, behind, 1)):
            arrived("agz", r % N, v["zr"].at[0])
            if h < 3:
                ring(r, 0, 64, device, r + step)
            else:
                ring(r, 0 if step < 0 else 32, 32, device, 4)
            pair(r)

    def g1(k):
        r = rel(k)
        own = (z + r) % N
        arrived("agc", r, v["zr"].at[0])
        for n in range(6):
            part = jnp.dot(v["nrm"][own], v["wup"][:, n * 256:n * 256 + 256], preferred_element_type=F32)
            first = n * 256
            f, b, first = ("paf", "pab", first) if first < CA else ("pbf", "pbb", first - CA)
            v[f][k, :, first:first + 256] = part
            v[b][k, :, first:first + 256] = part.astype(BF16)
        send("a1", k, v["pab"].at[k, rows((1 - xl) * 64, 64)], v["a1"].at[k], x_other)
        send("b1", k, v["pbb"].at[k, rows(y_far * 32, 16)], v["b1"].at[k, 0], above)
        send("b1", k, v["pbb"].at[k, rows(y_far * 32 + 16, 16)], v["b1"].at[k, 1], below)

    def s2(k):
        arrived("a1", k, v["a1"].at[k])
        mine = rows(xl * 64, 64)
        v["paf"][k, mine, :] = v["paf"][k, mine, :] + v["a1"][k].astype(F32)
        far = v["paf"][k, rows(xl * 64 + y_far * 16, 16), :].astype(BF16)
        v["fa"][k, 0] = far[:, :HA]
        v["fa"][k, 1] = far[:, HA:]
        send("a2", k, v["fa"].at[k, 0], v["a2"].at[k, 0], above)
        send("a2", k, v["fa"].at[k, 1], v["a2"].at[k, 1], below)
        arrived("b1", k, v["b1"].at[k])
        v["nb"][k, 0, :16] = (v["pbf"][k, rows(y_up * 32, 16), :] + v["b1"][k, 0].astype(F32)).astype(BF16)
        v["nb"][k, 0, 16:] = v["pbb"][k, rows(y_up * 32 + 16, 16), :]
        send("b2", k, v["nb"].at[k, 0], v["b2"].at[k, 0], above)
        v["nb"][k, 1, :16] = v["pbb"][k, rows(y_dn * 32, 16), :]
        v["nb"][k, 1, 16:] = (v["pbf"][k, rows(y_dn * 32 + 16, 16), :] + v["b1"][k, 1].astype(F32)).astype(BF16)
        send("b2", k, v["nb"].at[k, 1], v["b2"].at[k, 1], below)

    def s3(k):
        arrived("a2", k, v["a2"].at[k])
        up = v["paf"][k, rows(xl * 64 + y_up * 16, 16), :]
        v["na"][k, 0, :, :HA] = (up[:, :HA] + v["a2"][k, 0].astype(F32)).astype(BF16)
        v["na"][k, 0, :, HA:] = up[:, HA:].astype(BF16)
        send("a3", k, v["na"].at[k, 0], v["a3"].at[k, 0], above)
        down = v["paf"][k, rows(xl * 64 + y_dn * 16, 16), :]
        v["na"][k, 1, :, :HA] = down[:, :HA].astype(BF16)
        v["na"][k, 1, :, HA:] = (down[:, HA:] + v["a2"][k, 1].astype(F32)).astype(BF16)
        send("a3", k, v["na"].at[k, 1], v["a3"].at[k, 1], below)
        arrived("b2", k, v["b2"].at[k])
        mine = rows(y * 32, 32)
        v["pbf"][k, mine, :] = v["pbf"][k, mine, :] + v["b2"][k, 0].astype(F32) + v["b2"][k, 1].astype(F32)
        v["xb"][k] = v["pbf"][k, rows(y * 32 + (1 - xl) * 16, 16), :].astype(BF16)
        send("b3", k, v["xb"].at[k], v["b3"].at[k], x_other)

    def s4(k):
        arrived("a3", k, v["a3"].at[k])
        mine = rows(xl * 64 + y * 16, 16)
        total = v["paf"][k, mine, :] + v["a3"][k, 0].astype(F32) + v["a3"][k, 1].astype(F32)
        v["hida"][k, mine, :] = jnp.maximum(total + v["ubias"][:, :CA], 0.0).astype(BF16)
        here = v["hida"].at[k, mine]
        send("a4", k, here, here, above)
        send("a4", k, here, here, below)
        arrived("b3", k, v["b3"].at[k])
        mine = rows(y * 32 + xl * 16, 16)
        total = v["pbf"][k, mine, :] + v["b3"][k].astype(F32)
        v["hidb"][k, mine, :] = jnp.maximum(total + v["ubias"][:, CA:], 0.0).astype(BF16)
        here = v["hidb"].at[k, mine]
        send("b4", k, here, here, x_other)

    def s5(k):
        arrived("a4", k, v["a3"].at[k])
        here = v["hida"].at[k, rows(xl * 64 + y_dn * 16, 16), pl.ds(0, HA)]
        send("a5", k, here, here, above)
        here = v["hida"].at[k, rows(xl * 64 + y_up * 16, 16), pl.ds(HA, HA)]
        send("a5", k, here, here, below)
        arrived("b4", k, v["b3"].at[k])
        here = v["hidb"].at[k, rows(y * 32, 32)]
        send("b5", k, here, here, above)
        send("b5", k, here, here, below)

    def s6(k):
        arrived("a5", k, v["a2"].at[k])
        here = v["hida"].at[k, rows(xl * 64, 64)]
        send("a6", k, here, here, x_other)
        arrived("b5", k, v["b2"].at[k])
        here = v["hidb"].at[k, rows(y_dn * 32, 16)]
        send("b6", k, here, here, above)
        here = v["hidb"].at[k, rows(y_up * 32 + 16, 16)]
        send("b6", k, here, here, below)

    def g2(k):
        arrived("a6", k, v["a1"].at[k])
        arrived("b6", k, v["b1"].at[k])
        for n in range(6):
            cols = slice(n * 256, n * 256 + 256)
            v["pf"][k, :, cols] = jnp.dot(
                v["hida"][k], v["wdn"][:CA, cols], preferred_element_type=F32
            ) + jnp.dot(v["hidb"][k], v["wdn"][CA:, cols], preferred_element_type=F32)
        v["so"][k] = v["pf"][k, rows((1 - c) * 64, 64), :].astype(BF16)
        send("so", k, v["so"].at[k], v["sib"].at[k], sibling)

    def chip_sum(r, first=0, size=64):
        k = pos(r)
        return v["pf"][k, rows(c * 64 + first, size), :] + v["sib"][k, first:first + size].astype(F32)

    def scatter(h):
        if h == 4:
            arrived("so", pos(4), v["sib"].at[0])
            v["zs"][4] = chip_sum(4).astype(BF16)
            send("zr", 3, v["zs"].at[4, pl.ds(0, 32)], v["zr"].at[3, pl.ds(0, 32)], ahead)
            send("zr", 5, v["zs"].at[4, pl.ds(32, 32)], v["zr"].at[5, pl.ds(32, 32)], behind)
            return
        if h == 0:
            arrived("so", 0, v["sib"].at[0])
            arrived("zr", 0, v["zr"].at[0])
            arrived("zr", 4, v["zr"].at[4])
            total = v["xres"][...] + (chip_sum(0) + v["zr"][0].astype(F32) + v["zr"][4].astype(F32)) + v["dbias"][...]
            out[0] = total.astype(BF16)
            return
        for r, device, there in ((h, ahead, h - 1), (N - h, behind, (N - h + 1) % N or 4)):
            arrived("so", pos(r), v["sib"].at[0])
            if h == 3:
                first = 0 if r == 3 else 32
                arrived("zr", r, v["zr"].at[r, pl.ds(first, 32)])
                other = 32 - first
                v["zs"][r, first:first + 32] = (
                    chip_sum(r, first, 32) + v["zr"][r, first:first + 32].astype(F32)
                ).astype(BF16)
                v["zs"][r, other:other + 32] = chip_sum(r, other, 32).astype(BF16)
            else:
                arrived("zr", r, v["zr"].at[r])
                v["zs"][r] = (chip_sum(r) + v["zr"][r].astype(F32)).astype(BF16)
            send("zr", there, v["zs"].at[r], v["zr"].at[there], device)

    steps = dict(s2=s2, s3=s3, s4=s4, s5=s5, s6=s6, g2=g2)
    loads[5].wait()

    def slot(t, _):
        for name in ORDER:
            if name == "ag":
                for h, when in AG_SLOT.items():
                    pl.when(t == when)(functools.partial(gather, h))
            elif name == "z":
                for h, when in Z_SLOT.items():
                    pl.when(t == when)(functools.partial(scatter, h))
            elif name == "g1":
                pl.when(t < N)(functools.partial(g1, t))
            else:
                k = t - OFFSETS[name]
                pl.when((k >= 0) & (k < N))(functools.partial(steps[name], k))
        return 0

    loads[6].wait()
    lax.fori_loop(0, SLOTS, slot, 0)

    sent = dict(
        hand=v["hs"], agc=v["zr"], agz=v["zr"].at[pl.ds(0, 7)], a1=v["a1"], a2=v["a2"], a3=v["a3"],
        b1=v["b1"], b2=v["b2"], b3=v["b3"], a4=v["a3"], a5=v["a2"], a6=v["a1"], b4=v["b3"], b5=v["b2"],
        b6=v["b1"], so=v["sib"], zr=v["zr"].at[pl.ds(0, 7)],
    )
    for kind, like in sent.items():
        pltpu.make_async_copy(like, like, send_sem.at[SENDS.index(kind)]).wait()


def body(handoff, ln_gain, ln_bias, w_up, up_bias, w_down, down_bias):
    return pl.pallas_call(
        kernel,
        out_shape=jax.ShapeDtypeStruct((1, 64, W), BF16),
        in_specs=[pl.BlockSpec(memory_space=pl.ANY)] * 7,
        out_specs=pl.BlockSpec(memory_space=pltpu.VMEM),
        scratch_shapes=[pltpu.VMEM(shape, dtype) for shape, dtype in SCRATCH.values()] + [
            pltpu.SemaphoreType.DMA((7,)),
            pltpu.SemaphoreType.DMA,
            pltpu.SemaphoreType.DMA((len(SENDS),)),
            pltpu.SemaphoreType.DMA((len(RECVS), N)),
        ],
        compiler_params=pltpu.CompilerParams(
            collective_id=0, has_side_effects=True, vmem_limit_bytes=60 << 20
        ),
        name="relay_block",
    )(handoff, ln_gain, ln_bias, w_up, up_bias, w_down, down_bias)


def solution(mesh):
    placed = (
        P("section", ("mp", "dp"), None),
        P("section", "dp"),
        P("section", "dp"),
        P("section", "dp", "mp"),
        P("section", "mp"),
        P("section", "mp", "dp"),
        P("section", "dp"),
    )
    return jax.shard_map(
        body, mesh=mesh, in_specs=placed, out_specs=P("section", "mp", "dp"), check_vma=False
    )
```

time: 348 us -> 99 us (0.28)
  waiting for transfers between devices: 267 us -> 0 us
  Pallas kernels: 0 us -> 97.2 us
  blocking collectives: 33.9 us -> 0 us
  matrix products: 19.8 us -> 0 us
  between operations: 13.1 us -> 0.01 us
  starting transfers between devices: 7.47 us -> 0 us
  other arithmetic: 4.35 us -> 0 us
    psum x1 -> x0, waiting for transfers between devices: 148 us -> none  [body(): summed = lax.psum(pre, 'dp')]
    pallas_call x0 -> x1, Pallas kernels: none -> 97.2 us  [body(): pl.pallas_call(kernel, out_shape=jax.ShapeDtypeStruct((1, 64, W), BF16),...]
    reduce_scatter x1 -> x0, waiting for transfers between devices: 65.2 us -> none  [body(): lax.psum_scatter(jnp.dot(hidden, down_block, preferred_element_type=jnp.f...]
    all_gather x1 -> x0, waiting for transfers between devices: 42.3 us -> none  [body(): lax.all_gather(normed, 'mp', axis=0, tiled=True)]
    psum x2 -> x0, blocking collectives: 33.9 us -> none  [the longest x1 17.4 us: body(): total = lax.psum(jnp.sum(x, axis=1), 'dp')]
    dot_general x2 -> x0, matrix products: 19.8 us -> none  [the longest x1 10.1 us: body(): jnp.dot(hidden, down_block, preferred_element_type=jnp.float32)]
    ppermute x1 -> x0, waiting for transfers between devices: 6.22 us -> none  [shifted(): return lax.ppermute(value, axis, pairs)]
    all_to_all x1 -> x0, waiting for transfers between devices: 5.45 us -> none  [body(): lax.all_to_all(arrived, 'dp', split_axis=1, concat_axis=0, tiled=True)]
  transfers between devices with their start and end apart: 5 -> 0, of which waited for: 5 -> 0; matrix products, arithmetic and copies ran while one was open for 0% -> 0% of each run, Pallas kernels for 0% -> 0%
where the time goes in v1:
time: 99 us; the launch traced here: 98.9 us
  Pallas kernels  97.2 us (98%)
  local copies, waits for them, and re-layouts  1.62 us (2%)
    pallas_call x1, Pallas kernels, body(): pl.pallas_call(kernel, out_shape=jax.ShapeDtypeStruct((1, 64, W), BF16),...  97.2 us

profile of v1, /device:TPU:4, one launch (start us, length us, event | category | flops | bytes accessed | tf_op | source)
XLA Modules:
  0.0 98.9 jit_solution(4914482579827573768)
XLA Ops:
  0.0 97.2 %relay_block.1 = bf16[1,64,1536]{2,1,0:T(8,128)(2,1)} custom-call(bf16[1,8,12288]{2,1,0:T(8,128)(2,1)} %hand_in.1, f32[1,1536]{1,0:T(1,128)} %gain_in.1, f32[1,1536]{1,0:T(1,128)} %bias_in.1, bf16[1,1536,1536]{2,1,0:T(8,128)(2,1)} %wup_in.1, f32[1,1536]{1,0:T(1,128)} %ubias_in.1, bf16[1,1536,1536]{2,1,0:T(8,128)(2,1)} %wdn_in.1, f32[1,1536]{1,0:T(1,128)} %dbias_in.1), custom_call_target="tpu_custom_call" | custom-call | tf_op jit(solution)/shard_map/relay_block/pallas_call | solution.py:352
  97.2 1.6 %copy.9 = bf16[1,64,1536]{2,1,0:T(8,128)(2,1)} copy(bf16[1,64,1536]{2,1,0:T(8,128)(2,1)} %relay_block.1) | data formatting | bytes 393216

commit v2 on v0

v2 whole, which is shorter than its diff:
```python
import jax
import jax.numpy as jnp
from jax import lax
from jax.experimental import pallas as pl
from jax.experimental.pallas import tpu as pltpu
from jax.sharding import PartitionSpec as P

D = 12288
W = 1536
N = 8
CA = 896
CB = W - CA
F32 = jnp.float32
BF16 = jnp.bfloat16
MESH = pl.DeviceIdType.MESH

ORDER = (
    ("ga", 1, 0), ("ga", 7, 0), ("g1", 0, 0), ("ga", 7, 1), ("ga", 1, 1), ("g1", 7, 0), ("ga", 6, 0), ("ga", 2, 0),
    ("g1", 1, 0), ("s2a", 0, 0), ("ga", 6, 1), ("ga", 2, 1), ("g1", 6, 0), ("g1", 2, 0), ("ga", 5, 0), ("s2a", 7, 0),
    ("ga", 3, 0), ("ga", 3, 1), ("ga", 5, 1), ("g1", 3, 0), ("s2a", 1, 0), ("g1", 5, 0), ("ga", 4, 0), ("ga", 4, 1),
    ("g1", 4, 0), ("s2b", 3, 0), ("s2a", 2, 0), ("s2b", 6, 0), ("s2a", 3, 0), ("s2b", 2, 0), ("s2b", 5, 0),
    ("s2b", 0, 0), ("s2a", 6, 0), ("s2b", 4, 0), ("s2b", 7, 0), ("s2a", 4, 0), ("s2b", 1, 0), ("s2a", 5, 0),
    ("s4b", 6, 0), ("s4b", 3, 0), ("s4b", 2, 0), ("s4b", 0, 0), ("s4a", 3, 0), ("s4b", 4, 0), ("s4a", 2, 0),
    ("s4b", 5, 0), ("s4a", 4, 0), ("s4b", 7, 0), ("s4a", 5, 0), ("s6b", 4, 0), ("s4a", 6, 0), ("s6b", 3, 0),
    ("s6a", 3, 0), ("s6b", 5, 0), ("s6b", 6, 0), ("s4a", 7, 0), ("s4a", 1, 0), ("s6a", 4, 0), ("s4b", 1, 0),
    ("s6a", 5, 0), ("s6a", 6, 0), ("s6b", 2, 0), ("s6a", 2, 0), ("g2", 4, 0), ("g2", 3, 0), ("z4", 4, 0),
    ("g2", 5, 0), ("s4a", 0, 0), ("s6b", 7, 0), ("s6a", 7, 0), ("z", 3, 1), ("s6b", 1, 0), ("z", 5, 0), ("g2", 6, 0),
    ("z", 3, 0), ("s6a", 1, 0), ("z", 5, 1), ("g2", 2, 0), ("z", 6, 0), ("s6a", 0, 0), ("s6b", 0, 0), ("z", 2, 1),
    ("g2", 7, 0), ("z", 6, 1), ("z", 2, 0), ("g2", 1, 0), ("z", 7, 0), ("z", 1, 1), ("z", 7, 1), ("z", 1, 0),
    ("g2", 0, 0), ("z", 0, 1), ("z", 0, 0),
)

SCRATCH = dict(
    hand=((8, D), BF16),
    wup=((W, W), BF16),
    wdn=((W, W), BF16),
    gain=((1, W), F32),
    bias=((1, W), F32),
    ubias=((1, W), F32),
    dbias=((1, W), F32),
    hs=((8, 16, 896), BF16),
    hr=((8, 16, 896), BF16),
    xres=((64, W), F32),
    nrm=((N, 128, W), BF16),
    paf=((N, 128, CA), F32),
    pbf=((N, 128, CB), F32),
    pab=((N, 128, CA), BF16),
    pbb=((N, 128, CB), BF16),
    a1=((N, 64, CA), BF16),
    a2=((N, 3, 16, CA), BF16),
    b1=((N, 3, 32, CB), BF16),
    b2=((N, 16, CB), BF16),
    sa=((N, 64, CA), BF16),
    sb=((N, 16, CB), BF16),
    hid=((N, 128, W), BF16),
    pf=((N, 128, W), F32),
    so=((N, 64, W), BF16),
    sib=((N, 64, W), BF16),
    zs=((N, 64, W), BF16),
    zr=((N, 64, W), BF16),
)
SENDS = ("hand", "agc", "agz", "a1", "b1", "a2", "b2", "a3", "b3", "a4", "b4", "so", "zr")
RECVS = ("agc", "agz", "a1", "b1", "a2", "b2", "a3", "b3", "a4", "b4", "so", "zr")


def kernel(hand_in, gain_in, bias_in, wup_in, ubias_in, wdn_in, dbias_in, out, *refs):
    v = dict(zip(SCRATCH, refs))
    local_sem, hand_sem, send_sem, recv_sem = refs[len(SCRATCH):]
    s = lax.axis_index("section")
    d = lax.axis_index("dp")
    m = lax.axis_index("mp")
    xl, y, z, c = d // 4, d % 4, m // 2, m % 2
    other_y = [(y + j) % 4 for j in (1, 2, 3)]
    z_up, z_dn = (z + 1) % N, (z + N - 1) % N

    def at(section=s, x=xl, row=y, deep=z, core=c):
        return (section, x * 4 + row, deep * 2 + core)

    sibling = at(core=1 - c)
    x_other = at(x=1 - xl)
    in_row = [at(row=row) for row in other_y]
    ahead, behind = at(deep=z_up), at(deep=z_dn)

    loads = []
    for i, (src, dst) in enumerate((
        (hand_in, "hand"), (gain_in, None), (bias_in, None), (ubias_in, None), (dbias_in, None),
        (wup_in, "wup"), (wdn_in, "wdn"),
    )):
        name = ("hand", "gain", "bias", "ubias", "dbias", "wup", "wdn")[i]
        from_ref = src.at[0] if dst else src
        load = pltpu.make_async_copy(from_ref, v[name], local_sem.at[i])
        load.start()
        loads.append(load)

    barrier = pltpu.get_barrier_semaphore()
    others = [(1 - s, i, m) for i in range(8)]
    near = [sibling, x_other, *in_row, ahead, behind]
    for device in others + near:
        pl.semaphore_signal(barrier, inc=1, device_id=device, device_id_type=MESH)

    def send(kind, k, src, dst, device):
        pltpu.make_async_remote_copy(
            src_ref=src,
            dst_ref=dst,
            send_sem=send_sem.at[SENDS.index(kind)],
            recv_sem=recv_sem.at[RECVS.index(kind), k],
            device_id=device,
            device_id_type=MESH,
        ).start()

    def arrived(kind, k, like):
        pltpu.make_async_copy(like, like, recv_sem.at[RECVS.index(kind), k]).wait()

    def rows(start, size):
        return pl.ds(pl.multiple_of(start, 16), size)

    loads[0].wait()
    x = v["hand"][...].astype(F32)
    mean = jnp.sum(x, axis=1, keepdims=True) / D
    centred = x - mean
    rstd = lax.rsqrt(jnp.sum(centred * centred, axis=1, keepdims=True) / D + 1e-05)
    lane = lax.broadcasted_iota(jnp.int32, (8, 128), 1)

    def parts(value):
        high = value.astype(BF16).astype(F32)
        rest = value - high
        middle = rest.astype(BF16).astype(F32)
        low = rest - middle
        return jnp.where(lane < 32, high, jnp.where(lane < 64, middle, low))

    stats = jnp.concatenate([parts(mean), parts(rstd)], axis=0).astype(BF16)
    for i in range(8):
        left = x[:, i * W:i * W + 768]
        right = x[:, i * W + 768:(i + 1) * W]
        v["hs"][i, :, :768] = jnp.concatenate([left, right], axis=0).astype(BF16)
        v["hs"][i, :, 768:] = stats
    pl.semaphore_wait(barrier, len(others) + len(near))
    for i in range(8):
        pltpu.make_async_remote_copy(
            src_ref=v["hs"].at[i],
            dst_ref=v["hr"].at[d],
            send_sem=send_sem.at[0],
            recv_sem=hand_sem,
            device_id=others[i],
            device_id_type=MESH,
        ).start()
    for load in loads[1:5]:
        load.wait()
    pltpu.make_async_copy(v["hr"], v["hr"], hand_sem).wait()

    def unpack(i):
        held = v["hr"][i].astype(F32)
        stat = held[:, 768:]
        stat = stat[:, 0:1] + stat[:, 32:33] + stat[:, 64:65]
        return jnp.concatenate([held[:8, :768], held[8:, :768]], axis=1), stat[:8], stat[8:]

    def block(r, h):
        return v["nrm"].at[(z + r) % N, rows(c * 64 + h * 32, 32)]

    def pair(r, h):
        send("agc", r % N, block(r, h), block(r, h), sibling)

    def ring(r, h, step):
        send("agz", (r + step) % N * 2 + h, block(r, h), block(r, h), ahead if step < 0 else behind)

    for i in range(4):
        xa, mean_a, rstd_a = unpack(2 * i)
        xb, mean_b, rstd_b = unpack(2 * i + 1)
        two = jnp.concatenate([(xa - mean_a) * rstd_a, (xb - mean_b) * rstd_b], axis=0)
        v["nrm"][z, rows(c * 64 + i * 16, 16), :] = (two * v["gain"][...] + v["bias"][...]).astype(BF16)
        v["xres"][i * 16:i * 16 + 16, :] = jnp.concatenate([xa, xb], axis=0)
        if i % 2:
            ring(0, i // 2, -1)
            ring(0, i // 2, 1)
            pair(0, i // 2)

    def ga(r, h):
        arrived("agz", r * 2 + h, v["zr"].at[0, pl.ds(0, 32)])
        step = -1 if r > 4 else 1
        if r != 4 and (r + step != 4 or h == (0 if step < 0 else 1)):
            ring(r, h, step)
        pair(r, h)

    def g1(r):
        own = (z + r) % N
        arrived("agc", r, v["zr"].at[0])
        for n in range(0, W, 256):
            part = jnp.dot(v["nrm"][own], v["wup"][:, n:n + 256], preferred_element_type=F32)
            low = min(max(CA - n, 0), 256)
            if low:
                v["paf"][r, :, n:n + low] = part[:, :low]
                v["pab"][r, :, n:n + low] = part[:, :low].astype(BF16)
            if low < 256:
                v["pbf"][r, :, n + low - CA:n + 256 - CA] = part[:, low:]
                v["pbb"][r, :, n + low - CA:n + 256 - CA] = part[:, low:].astype(BF16)
        send("a1", r, v["pab"].at[r, rows((1 - xl) * 64, 64)], v["a1"].at[r], x_other)
        for j in (0, 2, 1):
            send("b1", r, v["pbb"].at[r, rows(other_y[j] * 32, 32)], v["b1"].at[r, j], in_row[j])

    def s2a(r):
        arrived("a1", r, v["a1"].at[r])
        total = v["paf"][r, rows(xl * 64, 64), :] + v["a1"][r].astype(F32)
        v["paf"][r, rows(xl * 64, 64), :] = total
        v["sa"][r] = total.astype(BF16)
        for j in (0, 2, 1):
            send("a2", r, v["sa"].at[r, rows(other_y[j] * 16, 16)], v["a2"].at[r, j], in_row[j])

    def s2b(r):
        arrived("b1", r, v["b1"].at[r])

        def total(x):
            sums = v["pbf"][r, rows(y * 32 + x * 16, 16), :]
            for j in range(3):
                sums = sums + v["b1"][r, j, rows(x * 16, 16), :].astype(F32)
            return sums

        v["sb"][r] = total(1 - xl).astype(BF16)
        send("b2", r, v["sb"].at[r], v["b2"].at[r], x_other)
        v["pbf"][r, rows(y * 32 + xl * 16, 16), :] = total(xl)

    def s4a(r):
        arrived("a2", r, v["a2"].at[r])
        mine = rows(xl * 64 + y * 16, 16)
        total = v["paf"][r, mine, :]
        for j in range(3):
            total = total + v["a2"][r, j].astype(F32)
        v["hid"][r, mine, :CA] = jnp.maximum(total + v["ubias"][:, :CA], 0.0).astype(BF16)
        here = v["hid"].at[r, mine, pl.ds(0, CA)]
        for j in (0, 2, 1):
            send("a3", r, here, here, in_row[j])

    def s4b(r):
        arrived("b2", r, v["b2"].at[r])
        mine = rows(y * 32 + xl * 16, 16)
        total = v["pbf"][r, mine, :] + v["b2"][r].astype(F32)
        v["hid"][r, mine, CA:] = jnp.maximum(total + v["ubias"][:, CA:], 0.0).astype(BF16)
        here = v["hid"].at[r, mine, pl.ds(CA, CB)]
        send("b3", r, here, here, x_other)

    def s6a(r):
        arrived("a3", r, v["a2"].at[r])
        here = v["hid"].at[r, rows(xl * 64, 64), pl.ds(0, CA)]
        send("a4", r, here, here, x_other)

    def s6b(r):
        arrived("b3", r, v["b2"].at[r])
        here = v["hid"].at[r, rows(y * 32, 32), pl.ds(CA, CB)]
        for j in (0, 2, 1):
            send("b4", r, here, here, in_row[j])

    def g2(r):
        arrived("a4", r, v["a1"].at[r])
        arrived("b4", r, v["b1"].at[r])
        for n in range(0, W, 256):
            v["pf"][r, :, n:n + 256] = jnp.dot(v["hid"][r], v["wdn"][:, n:n + 256], preferred_element_type=F32)
        v["so"][r] = v["pf"][r, rows((1 - c) * 64, 64), :].astype(BF16)
        send("so", r, v["so"].at[r], v["sib"].at[r], sibling)

    def chip_sum(r, h):
        return v["pf"][r, rows(c * 64 + h * 32, 32), :] + v["sib"][r, h * 32:h * 32 + 32].astype(F32)

    summed = set()

    def z_sum(r, h):
        if r not in summed:
            arrived("so", r, v["sib"].at[r])
            summed.add(r)
        half = pl.ds(h * 32, 32)
        total = chip_sum(r, h)
        if r in (1, 2, 6, 7) or (r, h) in ((3, 0), (5, 1)):
            arrived("zr", r * 2 + h, v["zr"].at[r, half])
            total = total + v["zr"][r, half].astype(F32)
        v["zs"][r, half] = total.astype(BF16)
        step = -1 if r < 4 or (r == 4 and h == 0) else 1
        there = (r + step) % N
        there = 4 if there == 0 and step > 0 else there
        send("zr", there * 2 + h, v["zs"].at[r, half], v["zr"].at[there, half], ahead if step < 0 else behind)

    def finish(h):
        if 0 not in summed:
            arrived("so", 0, v["sib"].at[0])
            summed.add(0)
        half = pl.ds(h * 32, 32)
        arrived("zr", h, v["zr"].at[0, half])
        arrived("zr", 8 + h, v["zr"].at[4, half])
        mixed = chip_sum(0, h) + v["zr"][0, half].astype(F32) + v["zr"][4, half].astype(F32)
        out[0, h * 32:h * 32 + 32] = (v["xres"][h * 32:h * 32 + 32] + mixed + v["dbias"][...]).astype(BF16)

    loads[5].wait()
    first_down = True
    chunk_steps = dict(g1=g1, s2a=s2a, s2b=s2b, s4a=s4a, s4b=s4b, s6a=s6a, s6b=s6b, g2=g2)
    for name, r, h in ORDER:
        if name == "g2" and first_down:
            loads[6].wait()
            first_down = False
        if name == "ga":
            ga(r, h)
        elif name == "z4":
            z_sum(4, 0)
            z_sum(4, 1)
        elif name == "z" and r == 0:
            finish(h)
        elif name == "z":
            z_sum(r, h)
        else:
            chunk_steps[name](r)

    sent = dict(
        hand=v["hs"], agc=v["zr"], agz=v["zr"].at[pl.ds(0, 7)], a1=v["a1"], b1=v["b1"], a2=v["a2"], b2=v["b2"],
        a3=v["a2"], b3=v["b2"], a4=v["a1"], b4=v["b1"], so=v["sib"], zr=v["zr"].at[pl.ds(0, 7)],
    )
    for kind, like in sent.items():
        pltpu.make_async_copy(like, like, send_sem.at[SENDS.index(kind)]).wait()


def body(handoff, ln_gain, ln_bias, w_up, up_bias, w_down, down_bias):
    return pl.pallas_call(
        kernel,
        out_shape=jax.ShapeDtypeStruct((1, 64, W), BF16),
        in_specs=[pl.BlockSpec(memory_space=pl.ANY)] * 7,
        out_specs=pl.BlockSpec(memory_space=pltpu.VMEM),
        scratch_shapes=[pltpu.VMEM(shape, dtype) for shape, dtype in SCRATCH.values()] + [
            pltpu.SemaphoreType.DMA((7,)),
            pltpu.SemaphoreType.DMA,
            pltpu.SemaphoreType.DMA((len(SENDS),)),
            pltpu.SemaphoreType.DMA((len(RECVS), 2 * N)),
        ],
        compiler_params=pltpu.CompilerParams(
            collective_id=0, has_side_effects=True, vmem_limit_bytes=60 << 20
        ),
        name="relay_block",
    )(handoff, ln_gain, ln_bias, w_up, up_bias, w_down, down_bias)


def solution(mesh):
    placed = (
        P("section", ("mp", "dp"), None),
        P("section", "dp"),
        P("section", "dp"),
        P("section", "dp", "mp"),
        P("section", "mp"),
        P("section", "mp", "dp"),
        P("section", "dp"),
    )
    return jax.shard_map(
        body, mesh=mesh, in_specs=placed, out_specs=P("section", "mp", "dp"), check_vma=False
    )
```

time: 348 us -> 86.3 us (0.25)
  waiting for transfers between devices: 267 us -> 0 us
  Pallas kernels: 0 us -> 84.3 us
  blocking collectives: 33.9 us -> 0 us
  matrix products: 19.8 us -> 0 us
  between operations: 13.1 us -> 0.01 us
  starting transfers between devices: 7.47 us -> 0 us
  other arithmetic: 4.35 us -> 0 us
    psum x1 -> x0, waiting for transfers between devices: 148 us -> none  [body(): summed = lax.psum(pre, 'dp')]
    pallas_call x0 -> x1, Pallas kernels: none -> 84.3 us  [body(): pl.pallas_call(kernel, out_shape=jax.ShapeDtypeStruct((1, 64, W), BF16),...]
    reduce_scatter x1 -> x0, waiting for transfers between devices: 65.2 us -> none  [body(): lax.psum_scatter(jnp.dot(hidden, down_block, preferred_element_type=jnp.f...]
    all_gather x1 -> x0, waiting for transfers between devices: 42.3 us -> none  [body(): lax.all_gather(normed, 'mp', axis=0, tiled=True)]
    psum x2 -> x0, blocking collectives: 33.9 us -> none  [the longest x1 17.4 us: body(): total = lax.psum(jnp.sum(x, axis=1), 'dp')]
    dot_general x2 -> x0, matrix products: 19.8 us -> none  [the longest x1 10.1 us: body(): jnp.dot(hidden, down_block, preferred_element_type=jnp.float32)]
    ppermute x1 -> x0, waiting for transfers between devices: 6.22 us -> none  [shifted(): return lax.ppermute(value, axis, pairs)]
    all_to_all x1 -> x0, waiting for transfers between devices: 5.45 us -> none  [body(): lax.all_to_all(arrived, 'dp', split_axis=1, concat_axis=0, tiled=True)]
  transfers between devices with their start and end apart: 5 -> 0, of which waited for: 5 -> 0; matrix products, arithmetic and copies ran while one was open for 0% -> 0% of each run, Pallas kernels for 0% -> 0%
where the time goes in v2:
time: 86.3 us; the launch traced here: 86 us
  Pallas kernels  84.3 us (98%)
  local copies, waits for them, and re-layouts  1.62 us (2%)
    pallas_call x1, Pallas kernels, body(): pl.pallas_call(kernel, out_shape=jax.ShapeDtypeStruct((1, 64, W), BF16),...  84.3 us

profile of v2, /device:TPU:4, one launch (start us, length us, event | category | flops | bytes accessed | tf_op | source)
XLA Modules:
  0.0 86.0 jit_solution(11481609373997466289)
XLA Ops:
  0.0 84.3 %relay_block.1 = bf16[1,64,1536]{2,1,0:T(8,128)(2,1)} custom-call(bf16[1,8,12288]{2,1,0:T(8,128)(2,1)} %hand_in.1, f32[1,1536]{1,0:T(1,128)} %gain_in.1, f32[1,1536]{1,0:T(1,128)} %bias_in.1, bf16[1,1536,1536]{2,1,0:T(8,128)(2,1)} %wup_in.1, f32[1,1536]{1,0:T(1,128)} %ubias_in.1, bf16[1,1536,1536]{2,1,0:T(8,128)(2,1)} %wdn_in.1, f32[1,1536]{1,0:T(1,128)} %dbias_in.1), custom_call_target="tpu_custom_call" | custom-call | tf_op jit(solution)/shard_map/relay_block/pallas_call | solution.py:317
  84.3 1.6 %copy.9 = bf16[1,64,1536]{2,1,0:T(8,128)(2,1)} copy(bf16[1,64,1536]{2,1,0:T(8,128)(2,1)} %relay_block.1) | data formatting | bytes 393216

commit v3 on v2

v3 whole, which is shorter than its diff:
```python
import jax
import jax.numpy as jnp
from jax import lax
from jax.experimental import pallas as pl
from jax.experimental.pallas import tpu as pltpu
from jax.sharding import PartitionSpec as P

D = 12288
W = 1536
N = 8
CA = 768
CB = W - CA
HA = CA // 2
CUTS = 4
PIECE = 64 // CUTS
DIRECT = ()
F32 = jnp.float32
BF16 = jnp.bfloat16
MESH = pl.DeviceIdType.MESH

ORDER = (
    ("n", 0, 0), ("n", 0, 1), ("n", 0, 2), ("n", 0, 3), ("ga", 1, 0), ("ga", 7, 0), ("ga", 1, 1), ("ga", 7, 1),
    ("g1", 0, 0), ("ga", 1, 2), ("ga", 7, 2), ("ga", 7, 3), ("ga", 1, 3), ("ga", 6, 0), ("ga", 2, 0), ("g1", 7, 0),
    ("ga", 2, 1), ("g1", 1, 0), ("ga", 6, 1), ("s2a", 0, 0), ("ga", 2, 2), ("s2b", 0, 0), ("ga", 2, 3), ("ga", 6, 2),
    ("ga", 6, 3), ("ga", 5, 0), ("s2b", 7, 0), ("g1", 2, 0), ("g1", 6, 0), ("ga", 3, 2), ("s2a", 7, 0), ("ga", 3, 1),
    ("ga", 5, 1), ("s2b", 1, 0), ("ga", 3, 0), ("ga", 3, 3), ("s2a", 1, 0), ("ga", 5, 3), ("ga", 5, 2), ("s3a", 0, 0),
    ("s2b", 2, 0), ("g1", 3, 0), ("ga", 4, 0), ("g1", 5, 0), ("ga", 4, 2), ("s2b", 6, 0), ("s2a", 2, 0),
    ("s3a", 7, 0), ("ga", 4, 1), ("ga", 4, 3), ("g1", 4, 0), ("s2b", 3, 0), ("s3b", 0, 0), ("s2a", 3, 0),
    ("s3a", 1, 0), ("s2a", 6, 0), ("s3a", 2, 0), ("s3b", 7, 0), ("s2b", 4, 0), ("s3b", 2, 0), ("s3b", 1, 0),
    ("s3b", 3, 0), ("s3a", 3, 0), ("s2a", 4, 0), ("s2b", 5, 0), ("s2a", 5, 0), ("s4a", 1, 0), ("s4b", 7, 0),
    ("s3b", 4, 0), ("s4b", 1, 0), ("s4a", 3, 0), ("s4b", 0, 0), ("s4b", 3, 0), ("s3a", 4, 0), ("s4a", 7, 0),
    ("s3a", 6, 0), ("s3b", 5, 0), ("s3a", 5, 0), ("s4a", 2, 0), ("s4b", 4, 0), ("s4b", 2, 0), ("s5a", 3, 0),
    ("s3b", 6, 0), ("s4a", 4, 0), ("s5b", 3, 0), ("s4a", 5, 0), ("s5b", 4, 0), ("s4b", 5, 0), ("s4b", 6, 0),
    ("s5a", 4, 0), ("s4a", 6, 0), ("s6a", 3, 0), ("s6b", 3, 0), ("s5a", 5, 0), ("s5b", 5, 0), ("s6b", 4, 0),
    ("s5a", 2, 0), ("s6a", 4, 0), ("s5a", 7, 0), ("s5b", 2, 0), ("s5a", 6, 0), ("s5b", 6, 0), ("s6a", 5, 0),
    ("s5a", 1, 0), ("g2", 3, 0), ("s6b", 5, 0), ("s6a", 2, 0), ("g2", 4, 0), ("z", 3, 2), ("s5b", 1, 0),
    ("s6a", 6, 0), ("s6b", 2, 0), ("s5b", 7, 0), ("s6a", 1, 0), ("z", 4, 0), ("z", 4, 2), ("g2", 5, 0), ("s6b", 6, 0),
    ("z", 4, 3), ("z", 4, 1), ("s4a", 0, 0), ("z", 3, 3), ("z", 5, 0), ("z", 5, 1), ("g2", 2, 0), ("s6a", 7, 0),
    ("z", 3, 0), ("z", 5, 2), ("s6b", 1, 0), ("s6b", 7, 0), ("s5b", 0, 0), ("g2", 6, 0), ("z", 5, 3), ("z", 3, 1),
    ("s5a", 0, 0), ("z", 2, 2), ("z", 6, 0), ("z", 2, 3), ("g2", 1, 0), ("z", 6, 1), ("z", 6, 2), ("z", 2, 0),
    ("g2", 7, 0), ("z", 6, 3), ("z", 2, 1), ("z", 1, 2), ("s6a", 0, 0), ("s6b", 0, 0), ("z", 7, 0), ("z", 1, 3),
    ("z", 7, 1), ("z", 7, 2), ("z", 1, 0), ("z", 7, 3), ("z", 1, 1), ("g2", 0, 0), ("z", 0, 1), ("z", 0, 0),
    ("z", 0, 2), ("z", 0, 3),
)

SCRATCH = dict(
    hand=((8, D), BF16),
    wup=((W, W), BF16),
    wdn=((W, W), BF16),
    gain=((1, W), F32),
    bias=((1, W), F32),
    ubias=((1, W), F32),
    dbias=((1, W), F32),
    hs=((8, 16, 896), BF16),
    hr=((8, 16, 896), BF16),
    xres=((64, W), F32),
    nrm=((N, 128, W), BF16),
    paf=((N, 128, CA), F32),
    pbf=((N, 128, CB), F32),
    pab=((N, 128, CA), BF16),
    pbb=((N, 128, CB), BF16),
    a1=((N, 64, CA), BF16),
    a2=((N, 2, 16, HA), BF16),
    a3=((N, 2, 16, CA), BF16),
    a2d=((N, 3, 16, CA), BF16),
    b1=((N, 2, 16, CB), BF16),
    b2=((N, 2, 32, CB), BF16),
    b1d=((N, 3, 32, CB), BF16),
    b3=((N, 16, CB), BF16),
    sa=((N, 64, CA), BF16),
    sa2=((N, 2, 16, CA), BF16),
    sb2=((N, 2, 32, CB), BF16),
    sb=((N, 16, CB), BF16),
    hid=((N, 128, W), BF16),
    pf=((N, 128, W), F32),
    so=((N, 64, W), BF16),
    sib=((N, 64, W), BF16),
    zs=((N, 64, W), BF16),
    zr=((N, 64, W), BF16),
)
KINDS = (
    "agc", "agz", "a1", "a2", "a3", "a2d", "b1", "b2", "b1d", "b3",
    "a4", "a5", "a3d", "a6", "b4", "b5", "b6", "b4d", "so", "zr",
)
SENDS = ("hand",) + KINDS
LANDINGS = 168


def kernel(hand_in, gain_in, bias_in, wup_in, ubias_in, wdn_in, dbias_in, out, *refs):
    v = dict(zip(SCRATCH, refs))
    local_sem, hand_sem, send_sem, recv_sem = refs[len(SCRATCH):]
    s = lax.axis_index("section")
    d = lax.axis_index("dp")
    m = lax.axis_index("mp")
    xl, y, z, c = d // 4, d % 4, m // 2, m % 2
    other_y = [(y + j) % 4 for j in (1, 2, 3)]
    z_up, z_dn = (z + 1) % N, (z + N - 1) % N

    def at(section=s, x=xl, row=y, deep=z, core=c):
        return (section, x * 4 + row, deep * 2 + core)

    sibling = at(core=1 - c)
    x_other = at(x=1 - xl)
    in_row = [at(row=row) for row in other_y]
    y_up, y_far, y_dn = other_y
    above, below = in_row[0], in_row[2]
    ahead, behind = at(deep=z_up), at(deep=z_dn)

    loads = []
    for i, (src, dst) in enumerate((
        (hand_in, "hand"), (gain_in, None), (bias_in, None), (ubias_in, None), (dbias_in, None),
        (wup_in, "wup"), (wdn_in, "wdn"),
    )):
        name = ("hand", "gain", "bias", "ubias", "dbias", "wup", "wdn")[i]
        from_ref = src.at[0] if dst else src
        load = pltpu.make_async_copy(from_ref, v[name], local_sem.at[i])
        load.start()
        loads.append(load)

    barrier = pltpu.get_barrier_semaphore()
    others = [(1 - s, i, m) for i in range(8)]
    near = [sibling, x_other, *in_row, ahead, behind]
    for device in others + near:
        pl.semaphore_signal(barrier, inc=1, device_id=device, device_id_type=MESH)

    slots = {}

    def landed(kind, k):
        return recv_sem.at[slots.setdefault((kind, k), len(slots))]

    def send(kind, k, src, dst, device):
        pltpu.make_async_remote_copy(
            src_ref=src,
            dst_ref=dst,
            send_sem=send_sem.at[SENDS.index(kind)],
            recv_sem=landed(kind, k),
            device_id=device,
            device_id_type=MESH,
        ).start()

    def arrived(kind, k, like):
        pltpu.make_async_copy(like, like, landed(kind, k)).wait()

    def rows(start, size):
        return pl.ds(pl.multiple_of(start, 16), size)

    loads[0].wait()
    x = v["hand"][...].astype(F32)
    mean = jnp.sum(x, axis=1, keepdims=True) / D
    centred = x - mean
    rstd = lax.rsqrt(jnp.sum(centred * centred, axis=1, keepdims=True) / D + 1e-05)
    lane = lax.broadcasted_iota(jnp.int32, (8, 128), 1)

    def parts(value):
        high = value.astype(BF16).astype(F32)
        rest = value - high
        middle = rest.astype(BF16).astype(F32)
        low = rest - middle
        return jnp.where(lane < 32, high, jnp.where(lane < 64, middle, low))

    stats = jnp.concatenate([parts(mean), parts(rstd)], axis=0).astype(BF16)
    for i in range(8):
        left = x[:, i * W:i * W + 768]
        right = x[:, i * W + 768:(i + 1) * W]
        v["hs"][i, :, :768] = jnp.concatenate([left, right], axis=0).astype(BF16)
        v["hs"][i, :, 768:] = stats
    pl.semaphore_wait(barrier, len(others) + len(near))
    def partner(step):
        low = 1 - d % 2 if step % 2 else d % 2
        return (d // 2 + step // 2) % 4 * 2 + low

    for i in range(8):
        other = partner(i)
        pltpu.make_async_remote_copy(
            src_ref=v["hs"].at[other],
            dst_ref=v["hr"].at[d],
            send_sem=send_sem.at[0],
            recv_sem=hand_sem.at[i // 2],
            device_id=(1 - s, other, m),
            device_id_type=MESH,
        ).start()
    for load in loads[1:5]:
        load.wait()

    def piece(p):
        return (d // 2 + 4 - p) % 4 * 16

    def unpack(i):
        held = v["hr"][i].astype(F32)
        stat = held[:, 768:]
        stat = stat[:, 0:1] + stat[:, 32:33] + stat[:, 64:65]
        return jnp.concatenate([held[:8, :768], held[8:, :768]], axis=1), stat[:8], stat[8:]

    def block(r, p):
        return v["nrm"].at[(z + r) % N, rows(c * 64 + piece(p), 16)]

    def pair(r, p):
        send("agc", r % N, block(r, p), block(r, p), sibling)

    def ring(r, h, step):
        send("agz", (r + step) % N * CUTS + h, block(r, h), block(r, h), ahead if step < 0 else behind)

    def normalize(p):
        pltpu.make_async_copy(v["hr"].at[pl.ds(0, 2)], v["hr"].at[pl.ds(0, 2)], hand_sem.at[p]).wait()
        first = piece(p) // 8
        xa, mean_a, rstd_a = unpack(first)
        xb, mean_b, rstd_b = unpack(first + 1)
        two = jnp.concatenate([(xa - mean_a) * rstd_a, (xb - mean_b) * rstd_b], axis=0)
        v["nrm"][z, rows(c * 64 + piece(p), 16), :] = (two * v["gain"][...] + v["bias"][...]).astype(BF16)
        v["xres"][rows(piece(p), 16), :] = jnp.concatenate([xa, xb], axis=0)
        ring(0, p, -1)
        ring(0, p, 1)
        pair(0, p)

    def ga(r, h):
        arrived("agz", r * CUTS + h, v["zr"].at[0, pl.ds(0, PIECE)])
        step = -1 if r > 4 else 1
        if r != 4 and (r + step != 4 or (h < CUTS // 2) == (step < 0)):
            ring(r, h, step)
        pair(r, h)

    def g1(r):
        own = (z + r) % N
        arrived("agc", r, v["zr"].at[0])
        for n in range(0, W, 256):
            part = jnp.dot(v["nrm"][own], v["wup"][:, n:n + 256], preferred_element_type=F32)
            f, b, first = ("paf", "pab", n) if n < CA else ("pbf", "pbb", n - CA)
            v[f][r, :, first:first + 256] = part
            v[b][r, :, first:first + 256] = part.astype(BF16)
        send("a1", r, v["pab"].at[r, rows((1 - xl) * 64, 64)], v["a1"].at[r], x_other)
        if r in DIRECT:
            for j in (0, 2, 1):
                send("b1d", r, v["pbb"].at[r, rows(other_y[j] * 32, 32)], v["b1d"].at[r, j], in_row[j])
        else:
            send("b1", r, v["pbb"].at[r, rows(y_far * 32, 16)], v["b1"].at[r, 0], above)
            send("b1", r, v["pbb"].at[r, rows(y_far * 32 + 16, 16)], v["b1"].at[r, 1], below)

    def s2a(r):
        arrived("a1", r, v["a1"].at[r])
        total = v["paf"][r, rows(xl * 64, 64), :] + v["a1"][r].astype(F32)
        v["paf"][r, rows(xl * 64, 64), :] = total
        v["sa"][r] = total.astype(BF16)
        if r in DIRECT:
            for j in (0, 2, 1):
                send("a2d", r, v["sa"].at[r, rows(other_y[j] * 16, 16)], v["a2d"].at[r, j], in_row[j])
        else:
            far = rows(y_far * 16, 16)
            send("a2", r, v["sa"].at[r, far, pl.ds(0, HA)], v["a2"].at[r, 0], above)
            send("a2", r, v["sa"].at[r, far, pl.ds(HA, HA)], v["a2"].at[r, 1], below)

    def x_sums(r, kind):
        def total(x):
            sums = v["pbf"][r, rows(y * 32 + x * 16, 16), :]
            for j in range(3 if kind == "b1d" else 2):
                sums = sums + v[kind][r, j, rows(x * 16, 16), :].astype(F32)
            return sums

        v["sb"][r] = total(1 - xl).astype(BF16)
        send("b3", r, v["sb"].at[r], v["b3"].at[r], x_other)
        v["pbf"][r, rows(y * 32 + xl * 16, 16), :] = total(xl)

    def s2b(r):
        if r in DIRECT:
            arrived("b1d", r, v["b1d"].at[r])
            x_sums(r, "b1d")
            return
        arrived("b1", r, v["b1"].at[r])
        up, down = rows(y_up * 32, 16), rows(y_dn * 32 + 16, 16)
        v["sb2"][r, 0, :16] = (v["pbf"][r, up, :] + v["b1"][r, 0].astype(F32)).astype(BF16)
        v["sb2"][r, 0, 16:] = v["pbb"][r, rows(y_up * 32 + 16, 16), :]
        send("b2", r, v["sb2"].at[r, 0], v["b2"].at[r, 0], above)
        v["sb2"][r, 1, :16] = v["pbb"][r, rows(y_dn * 32, 16), :]
        v["sb2"][r, 1, 16:] = (v["pbf"][r, down, :] + v["b1"][r, 1].astype(F32)).astype(BF16)
        send("b2", r, v["sb2"].at[r, 1], v["b2"].at[r, 1], below)

    def s3a(r):
        arrived("a2", r, v["a2"].at[r])
        up = v["paf"][r, rows(xl * 64 + y_up * 16, 16), :]
        v["sa2"][r, 0, :, :HA] = (up[:, :HA] + v["a2"][r, 0].astype(F32)).astype(BF16)
        v["sa2"][r, 0, :, HA:] = up[:, HA:].astype(BF16)
        send("a3", r, v["sa2"].at[r, 0], v["a3"].at[r, 0], above)
        down = v["paf"][r, rows(xl * 64 + y_dn * 16, 16), :]
        v["sa2"][r, 1, :, :HA] = down[:, :HA].astype(BF16)
        v["sa2"][r, 1, :, HA:] = (down[:, HA:] + v["a2"][r, 1].astype(F32)).astype(BF16)
        send("a3", r, v["sa2"].at[r, 1], v["a3"].at[r, 1], below)

    def s3b(r):
        arrived("b2", r, v["b2"].at[r])
        x_sums(r, "b2")

    def s4a(r):
        kind = "a2d" if r in DIRECT else "a3"
        arrived(kind, r, v[kind].at[r])
        mine = rows(xl * 64 + y * 16, 16)
        total = v["paf"][r, mine, :]
        for j in range(3 if r in DIRECT else 2):
            total = total + v[kind][r, j].astype(F32)
        v["hid"][r, mine, :CA] = jnp.maximum(total + v["ubias"][:, :CA], 0.0).astype(BF16)
        here = v["hid"].at[r, mine, pl.ds(0, CA)]
        if r in DIRECT:
            for j in (0, 2, 1):
                send("a3d", r, here, here, in_row[j])
        else:
            send("a4", r, here, here, above)
            send("a4", r, here, here, below)

    def s4b(r):
        arrived("b3", r, v["b3"].at[r])
        mine = rows(y * 32 + xl * 16, 16)
        total = v["pbf"][r, mine, :] + v["b3"][r].astype(F32)
        v["hid"][r, mine, CA:] = jnp.maximum(total + v["ubias"][:, CA:], 0.0).astype(BF16)
        here = v["hid"].at[r, mine, pl.ds(CA, CB)]
        send("b4", r, here, here, x_other)

    def s5a(r):
        arrived("a4", r, v["a3"].at[r])
        here = v["hid"].at[r, rows(xl * 64 + y_dn * 16, 16), pl.ds(0, HA)]
        send("a5", r, here, here, above)
        here = v["hid"].at[r, rows(xl * 64 + y_up * 16, 16), pl.ds(HA, HA)]
        send("a5", r, here, here, below)

    def y_back(r):
        arrived("b4", r, v["b3"].at[r])
        here = v["hid"].at[r, rows(y * 32, 32), pl.ds(CA, CB)]
        if r in DIRECT:
            for j in (0, 2, 1):
                send("b4d", r, here, here, in_row[j])
        else:
            send("b5", r, here, here, above)
            send("b5", r, here, here, below)

    def s5b(r):
        y_back(r)

    def s6a(r):
        if r in DIRECT:
            arrived("a3d", r, v["a2d"].at[r])
        else:
            arrived("a5", r, v["a2"].at[r])
        here = v["hid"].at[r, rows(xl * 64, 64), pl.ds(0, CA)]
        send("a6", r, here, here, x_other)

    def s6b(r):
        if r in DIRECT:
            y_back(r)
            return
        arrived("b5", r, v["b2"].at[r])
        here = v["hid"].at[r, rows(y_dn * 32, 16), pl.ds(CA, CB)]
        send("b6", r, here, here, above)
        here = v["hid"].at[r, rows(y_up * 32 + 16, 16), pl.ds(CA, CB)]
        send("b6", r, here, here, below)

    def g2(r):
        arrived("a6", r, v["a1"].at[r])
        if r in DIRECT:
            arrived("b4d", r, v["b1d"].at[r])
        else:
            arrived("b6", r, v["b1"].at[r])
        for n in range(0, W, 256):
            v["pf"][r, :, n:n + 256] = jnp.dot(v["hid"][r], v["wdn"][:, n:n + 256], preferred_element_type=F32)
        v["so"][r] = v["pf"][r, rows((1 - c) * 64, 64), :].astype(BF16)
        send("so", r, v["so"].at[r], v["sib"].at[r], sibling)

    def chip_sum(r, h):
        return v["pf"][r, rows(c * 64 + h * PIECE, PIECE), :] + v["sib"][r, h * PIECE:(h + 1) * PIECE].astype(F32)

    summed = set()

    def z_sum(r, h):
        if r not in summed:
            arrived("so", r, v["sib"].at[r])
            summed.add(r)
        part = pl.ds(h * PIECE, PIECE)
        total = chip_sum(r, h)
        if r in (1, 2, 6, 7) or (r == 3 and h < CUTS // 2) or (r == 5 and h >= CUTS // 2):
            arrived("zr", r * CUTS + h, v["zr"].at[r, part])
            total = total + v["zr"][r, part].astype(F32)
        v["zs"][r, part] = total.astype(BF16)
        step = -1 if r < 4 or (r == 4 and h < CUTS // 2) else 1
        there = (r + step) % N
        there = 4 if there == 0 and step > 0 else there
        send("zr", there * CUTS + h, v["zs"].at[r, part], v["zr"].at[there, part], ahead if step < 0 else behind)

    def finish(h):
        if 0 not in summed:
            arrived("so", 0, v["sib"].at[0])
            summed.add(0)
        part = pl.ds(h * PIECE, PIECE)
        arrived("zr", h, v["zr"].at[0, part])
        arrived("zr", 4 * CUTS + h, v["zr"].at[4, part])
        mixed = chip_sum(0, h) + v["zr"][0, part].astype(F32) + v["zr"][4, part].astype(F32)
        out[0, h * PIECE:(h + 1) * PIECE] = (v["xres"][h * PIECE:(h + 1) * PIECE] + mixed + v["dbias"][...]).astype(BF16)

    first_down = True
    chunk_steps = dict(
        g1=g1, s2a=s2a, s2b=s2b, s3a=s3a, s3b=s3b, s4a=s4a, s4b=s4b, s5a=s5a, s5b=s5b, s6a=s6a, s6b=s6b, g2=g2
    )
    first_up = True
    for name, r, h in ORDER:
        if name == "g1" and first_up:
            loads[5].wait()
            first_up = False
        if name == "g2" and first_down:
            loads[6].wait()
            first_down = False
        if name == "ga":
            ga(r, h)
        elif name == "n":
            normalize(h)
        elif name == "z" and r == 0:
            finish(h)
        elif name == "z":
            z_sum(r, h)
        else:
            chunk_steps[name](r)

    sent = dict(
        hand=v["hs"], agc=v["zr"], agz=v["zr"].at[pl.ds(0, 7)], a1=v["a1"], a6=v["a1"], b3=v["b3"], b4=v["b3"],
        so=v["sib"], zr=v["zr"].at[pl.ds(0, 7)],
    )
    by_ring = pl.ds(0, N - len(DIRECT))
    for kind, like in dict(a2="a2", a3="a3", b1="b1", b2="b2", a4="a3", a5="a2", b5="b2", b6="b1").items():
        if len(DIRECT) < N:
            sent[kind] = v[like].at[by_ring]
    for kind, like in dict(a2d="a2d", b1d="b1d", a3d="a2d", b4d="b1d").items():
        if DIRECT:
            sent[kind] = v[like].at[pl.ds(0, len(DIRECT))]
    for kind, like in sent.items():
        pltpu.make_async_copy(like, like, send_sem.at[SENDS.index(kind)]).wait()


def body(handoff, ln_gain, ln_bias, w_up, up_bias, w_down, down_bias):
    return pl.pallas_call(
        kernel,
        out_shape=jax.ShapeDtypeStruct((1, 64, W), BF16),
        in_specs=[pl.BlockSpec(memory_space=pl.ANY)] * 7,
        out_specs=pl.BlockSpec(memory_space=pltpu.VMEM),
        scratch_shapes=[pltpu.VMEM(shape, dtype) for shape, dtype in SCRATCH.values()] + [
            pltpu.SemaphoreType.DMA((7,)),
            pltpu.SemaphoreType.DMA((4,)),
            pltpu.SemaphoreType.DMA((len(SENDS),)),
            pltpu.SemaphoreType.DMA((LANDINGS,)),
        ],
        compiler_params=pltpu.CompilerParams(
            collective_id=0, has_side_effects=True, vmem_limit_bytes=60 << 20
        ),
        name="relay_block",
    )(handoff, ln_gain, ln_bias, w_up, up_bias, w_down, down_bias)


def solution(mesh):
    placed = (
        P("section", ("mp", "dp"), None),
        P("section", "dp"),
        P("section", "dp"),
        P("section", "dp", "mp"),
        P("section", "mp"),
        P("section", "mp", "dp"),
        P("section", "dp"),
    )
    return jax.shard_map(
        body, mesh=mesh, in_specs=placed, out_specs=P("section", "mp", "dp"), check_vma=False
    )
```

time: 86.3 us -> 82.5 us (0.956)
  Pallas kernels: 84.3 us -> 80.8 us
    pallas_call x1, Pallas kernels: 84.3 us -> 80.8 us  [body(): pl.pallas_call(kernel, out_shape=jax.ShapeDtypeStruct((1, 64, W), BF16),...]
where the time goes in v3:
time: 82.5 us; the launch traced here: 82.4 us
  Pallas kernels  80.8 us (98%)
  local copies, waits for them, and re-layouts  1.62 us (2%)
    pallas_call x1, Pallas kernels, body(): pl.pallas_call(kernel, out_shape=jax.ShapeDtypeStruct((1, 64, W), BF16),...  80.8 us

profile of v3, /device:TPU:4, one launch (start us, length us, event | category | flops | bytes accessed | tf_op | source)
XLA Modules:
  0.0 82.4 jit_solution(6822126351190739773)
XLA Ops:
  0.0 80.8 %relay_block.1 = bf16[1,64,1536]{2,1,0:T(8,128)(2,1)} custom-call(bf16[1,8,12288]{2,1,0:T(8,128)(2,1)} %hand_in.1, f32[1,1536]{1,0:T(1,128)} %gain_in.1, f32[1,1536]{1,0:T(1,128)} %bias_in.1, bf16[1,1536,1536]{2,1,0:T(8,128)(2,1)} %wup_in.1, f32[1,1536]{1,0:T(1,128)} %ubias_in.1, bf16[1,1536,1536]{2,1,0:T(8,128)(2,1)} %wdn_in.1, f32[1,1536]{1,0:T(1,128)} %dbias_in.1), custom_call_target="tpu_custom_call" | custom-call | tf_op jit(solution)/shard_map/relay_block/pallas_call | solution.py:433
  80.8 1.6 %copy.9 = bf16[1,64,1536]{2,1,0:T(8,128)(2,1)} copy(bf16[1,64,1536]{2,1,0:T(8,128)(2,1)} %relay_block.1) | data formatting | bytes 393216

commit v4 on v3

v4 whole, which is shorter than its diff:
```python
import types

import jax
import jax.numpy as jnp
from jax import lax
from jax.experimental import pallas as pl
from jax.experimental.pallas import tpu as pltpu
from jax.sharding import PartitionSpec as P

D = 12288
W = 1536
N = 8
CA = 768
CB = W - CA
HA = CA // 2
CUTS = 4
PIECE = 64 // CUTS
DIRECT = ()
F32 = jnp.float32
BF16 = jnp.bfloat16
MESH = pl.DeviceIdType.MESH

N_, GA_, G1_, S2A_, S2B_, S3A_, S3B_, S4A_, S4B_, S5A_, S5B_, S6A_, S6B_, G2_, Z_ = range(15)
ORDER = (
    (N_, 0, 0), (N_, 0, 1), (N_, 0, 2), (N_, 0, 3), (GA_, 1, 0), (GA_, 7, 0), (GA_, 1, 1), (GA_, 7, 1), (G1_, 0, 0),
    (GA_, 1, 2), (GA_, 7, 2), (GA_, 7, 3), (GA_, 1, 3), (GA_, 6, 0), (GA_, 2, 0), (G1_, 7, 0), (GA_, 2, 1),
    (G1_, 1, 0), (GA_, 6, 1), (S2A_, 0, 0), (GA_, 2, 2), (S2B_, 0, 0), (GA_, 2, 3), (GA_, 6, 2), (GA_, 6, 3),
    (GA_, 5, 0), (S2B_, 7, 0), (G1_, 2, 0), (G1_, 6, 0), (GA_, 3, 2), (S2A_, 7, 0), (GA_, 3, 1), (GA_, 5, 1),
    (S2B_, 1, 0), (GA_, 3, 0), (GA_, 3, 3), (S2A_, 1, 0), (GA_, 5, 3), (GA_, 5, 2), (S3A_, 0, 0), (S2B_, 2, 0),
    (G1_, 3, 0), (GA_, 4, 0), (G1_, 5, 0), (GA_, 4, 2), (S2B_, 6, 0), (S2A_, 2, 0), (S3A_, 7, 0), (GA_, 4, 1),
    (GA_, 4, 3), (G1_, 4, 0), (S2B_, 3, 0), (S3B_, 0, 0), (S2A_, 3, 0), (S3A_, 1, 0), (S2A_, 6, 0), (S3A_, 2, 0),
    (S3B_, 7, 0), (S2B_, 4, 0), (S3B_, 2, 0), (S3B_, 1, 0), (S3B_, 3, 0), (S3A_, 3, 0), (S2A_, 4, 0), (S2B_, 5, 0),
    (S2A_, 5, 0), (S4A_, 1, 0), (S4B_, 7, 0), (S3B_, 4, 0), (S4B_, 1, 0), (S4A_, 3, 0), (S4B_, 0, 0), (S4B_, 3, 0),
    (S3A_, 4, 0), (S4A_, 7, 0), (S3A_, 6, 0), (S3B_, 5, 0), (S3A_, 5, 0), (S4A_, 2, 0), (S4B_, 4, 0), (S4B_, 2, 0),
    (S5A_, 3, 0), (S3B_, 6, 0), (S4A_, 4, 0), (S5B_, 3, 0), (S4A_, 5, 0), (S5B_, 4, 0), (S4B_, 5, 0), (S4B_, 6, 0),
    (S5A_, 4, 0), (S4A_, 6, 0), (S6A_, 3, 0), (S6B_, 3, 0), (S5A_, 5, 0), (S5B_, 5, 0), (S6B_, 4, 0), (S5A_, 2, 0),
    (S6A_, 4, 0), (S5A_, 7, 0), (S5B_, 2, 0), (S5A_, 6, 0), (S5B_, 6, 0), (S6A_, 5, 0), (S5A_, 1, 0), (G2_, 3, 0),
    (S6B_, 5, 0), (S6A_, 2, 0), (G2_, 4, 0), (Z_, 3, 2), (S5B_, 1, 0), (S6A_, 6, 0), (S6B_, 2, 0), (S5B_, 7, 0),
    (S6A_, 1, 0), (Z_, 4, 0), (Z_, 4, 2), (G2_, 5, 0), (S6B_, 6, 0), (Z_, 4, 3), (Z_, 4, 1), (S4A_, 0, 0), (Z_, 3, 3),
    (Z_, 5, 0), (Z_, 5, 1), (G2_, 2, 0), (S6A_, 7, 0), (Z_, 3, 0), (Z_, 5, 2), (S6B_, 1, 0), (S6B_, 7, 0),
    (S5B_, 0, 0), (G2_, 6, 0), (Z_, 5, 3), (Z_, 3, 1), (S5A_, 0, 0), (Z_, 2, 2), (Z_, 6, 0), (Z_, 2, 3), (G2_, 1, 0),
    (Z_, 6, 1), (Z_, 6, 2), (Z_, 2, 0), (G2_, 7, 0), (Z_, 6, 3), (Z_, 2, 1), (Z_, 1, 2), (S6A_, 0, 0), (S6B_, 0, 0),
    (Z_, 7, 0), (Z_, 1, 3), (Z_, 7, 1), (Z_, 7, 2), (Z_, 1, 0), (Z_, 7, 3), (Z_, 1, 1), (G2_, 0, 0), (Z_, 0, 1),
    (Z_, 0, 0), (Z_, 0, 2), (Z_, 0, 3),
)

SCRATCH = dict(
    hand=((8, D), BF16),
    wup=((W, W), BF16),
    wdn=((W, W), BF16),
    gain=((1, W), F32),
    bias=((1, W), F32),
    ubias=((1, W), F32),
    dbias=((1, W), F32),
    hs=((8, 16, 896), BF16),
    hr=((8, 16, 896), BF16),
    xres=((64, W), F32),
    nrm=((N, 128, W), BF16),
    paf=((N, 128, CA), F32),
    pbf=((N, 128, CB), F32),
    pab=((N, 128, CA), BF16),
    pbb=((N, 128, CB), BF16),
    a1=((N, 64, CA), BF16),
    a2=((N, 2, 16, HA), BF16),
    a3=((N, 2, 16, CA), BF16),
    a2d=((N, 3, 16, CA), BF16),
    b1=((N, 2, 16, CB), BF16),
    b2=((N, 2, 32, CB), BF16),
    b1d=((N, 3, 32, CB), BF16),
    b3=((N, 16, CB), BF16),
    sa=((N, 64, CA), BF16),
    sa2=((N, 2, 16, CA), BF16),
    sb2=((N, 2, 32, CB), BF16),
    sb=((N, 16, CB), BF16),
    hid=((N, 128, W), BF16),
    pf=((N, 128, W), F32),
    so=((N, 64, W), BF16),
    sib=((N, 64, W), BF16),
    zs=((N, 64, W), BF16),
    zr=((N, 64, W), BF16),
)
KINDS = (
    "agc", "agz", "a1", "a2", "a3", "a2d", "b1", "b2", "b1d", "b3",
    "a4", "a5", "a3d", "a6", "b4", "b5", "b6", "b4d", "so", "zr",
)
SENDS = ("hand",) + KINDS
LANDINGS = 168


def kernel(hand_in, gain_in, bias_in, wup_in, ubias_in, wdn_in, dbias_in, out, *refs):
    named = dict(zip(SCRATCH, refs))
    v = types.SimpleNamespace(**named)
    local_sem, hand_sem, send_sem, recv_sem = refs[len(SCRATCH):]
    s = lax.axis_index("section")
    d = lax.axis_index("dp")
    m = lax.axis_index("mp")
    xl, y, z, c = d // 4, d % 4, m // 2, m % 2
    other_y = [(y + j) % 4 for j in (1, 2, 3)]
    z_up, z_dn = (z + 1) % N, (z + N - 1) % N

    def at(section=s, x=xl, row=y, deep=z, core=c):
        return (section, x * 4 + row, deep * 2 + core)

    sibling = at(core=1 - c)
    x_other = at(x=1 - xl)
    in_row = [at(row=row) for row in other_y]
    y_up, y_far, y_dn = other_y
    above, below = in_row[0], in_row[2]
    ahead, behind = at(deep=z_up), at(deep=z_dn)

    loads = []
    for i, (src, dst) in enumerate((
        (hand_in, "hand"), (gain_in, None), (bias_in, None), (ubias_in, None), (dbias_in, None),
        (wup_in, "wup"), (wdn_in, "wdn"),
    )):
        name = ("hand", "gain", "bias", "ubias", "dbias", "wup", "wdn")[i]
        from_ref = src.at[0] if dst else src
        load = pltpu.make_async_copy(from_ref, named[name], local_sem.at[i])
        load.start()
        loads.append(load)

    barrier = pltpu.get_barrier_semaphore()
    others = [(1 - s, i, m) for i in range(8)]
    near = [sibling, x_other, *in_row, ahead, behind]
    for device in others + near:
        pl.semaphore_signal(barrier, inc=1, device_id=device, device_id_type=MESH)

    slots = {}

    def landed(kind, k):
        return recv_sem.at[slots.setdefault((kind, k), len(slots))]

    def send(kind, k, src, dst, device):
        pltpu.make_async_remote_copy(
            src_ref=src,
            dst_ref=dst,
            send_sem=send_sem.at[SENDS.index(kind)],
            recv_sem=landed(kind, k),
            device_id=device,
            device_id_type=MESH,
        ).start()

    def arrived(kind, k, like):
        pltpu.make_async_copy(like, like, landed(kind, k)).wait()

    def rows(start, size):
        return pl.ds(pl.multiple_of(start, 16), size)

    loads[0].wait()
    x = v.hand[...].astype(F32)
    mean = jnp.sum(x, axis=1, keepdims=True) / D
    centred = x - mean
    rstd = lax.rsqrt(jnp.sum(centred * centred, axis=1, keepdims=True) / D + 1e-05)
    lane = lax.broadcasted_iota(jnp.int32, (8, 128), 1)

    def parts(value):
        high = value.astype(BF16).astype(F32)
        rest = value - high
        middle = rest.astype(BF16).astype(F32)
        low = rest - middle
        return jnp.where(lane < 32, high, jnp.where(lane < 64, middle, low))

    stats = jnp.concatenate([parts(mean), parts(rstd)], axis=0).astype(BF16)
    for i in range(8):
        left = x[:, i * W:i * W + 768]
        right = x[:, i * W + 768:(i + 1) * W]
        v.hs[i, :, :768] = jnp.concatenate([left, right], axis=0).astype(BF16)
        v.hs[i, :, 768:] = stats
    pl.semaphore_wait(barrier, len(others) + len(near))
    def partner(step):
        low = 1 - d % 2 if step % 2 else d % 2
        return (d // 2 + step // 2) % 4 * 2 + low

    for i in range(8):
        other = partner(i)
        pltpu.make_async_remote_copy(
            src_ref=v.hs.at[other],
            dst_ref=v.hr.at[d],
            send_sem=send_sem.at[0],
            recv_sem=hand_sem.at[i // 2],
            device_id=(1 - s, other, m),
            device_id_type=MESH,
        ).start()
    for load in loads[1:5]:
        load.wait()

    def piece(p):
        return (d // 2 + 4 - p) % 4 * 16

    def unpack(i):
        held = v.hr[i].astype(F32)
        stat = held[:, 768:]
        stat = stat[:, 0:1] + stat[:, 32:33] + stat[:, 64:65]
        return jnp.concatenate([held[:8, :768], held[8:, :768]], axis=1), stat[:8], stat[8:]

    def block(r, p):
        return v.nrm.at[(z + r) % N, rows(c * 64 + piece(p), 16)]

    def pair(r, p):
        send("agc", r % N, block(r, p), block(r, p), sibling)

    def ring(r, h, step):
        send("agz", (r + step) % N * CUTS + h, block(r, h), block(r, h), ahead if step < 0 else behind)

    def normalize(p):
        pltpu.make_async_copy(v.hr.at[pl.ds(0, 2)], v.hr.at[pl.ds(0, 2)], hand_sem.at[p]).wait()
        first = piece(p) // 8
        xa, mean_a, rstd_a = unpack(first)
        xb, mean_b, rstd_b = unpack(first + 1)
        two = jnp.concatenate([(xa - mean_a) * rstd_a, (xb - mean_b) * rstd_b], axis=0)
        v.nrm[z, rows(c * 64 + piece(p), 16), :] = (two * v.gain[...] + v.bias[...]).astype(BF16)
        v.xres[rows(piece(p), 16), :] = jnp.concatenate([xa, xb], axis=0)
        ring(0, p, -1)
        ring(0, p, 1)
        pair(0, p)

    def ga(r, h):
        arrived("agz", r * CUTS + h, v.zr.at[0, pl.ds(0, PIECE)])
        step = -1 if r > 4 else 1
        if r != 4 and (r + step != 4 or (h < CUTS // 2) == (step < 0)):
            ring(r, h, step)
        pair(r, h)

    def g1(r):
        own = (z + r) % N
        arrived("agc", r, v.zr.at[0])
        for n in range(0, W, 256):
            part = jnp.dot(v.nrm[own], v.wup[:, n:n + 256], preferred_element_type=F32)
            f, b, first = ("paf", "pab", n) if n < CA else ("pbf", "pbb", n - CA)
            named[f][r, :, first:first + 256] = part
            named[b][r, :, first:first + 256] = part.astype(BF16)
        send("a1", r, v.pab.at[r, rows((1 - xl) * 64, 64)], v.a1.at[r], x_other)
        if r in DIRECT:
            for j in (0, 2, 1):
                send("b1d", r, v.pbb.at[r, rows(other_y[j] * 32, 32)], v.b1d.at[r, j], in_row[j])
        else:
            send("b1", r, v.pbb.at[r, rows(y_far * 32, 16)], v.b1.at[r, 0], above)
            send("b1", r, v.pbb.at[r, rows(y_far * 32 + 16, 16)], v.b1.at[r, 1], below)

    def s2a(r):
        arrived("a1", r, v.a1.at[r])
        total = v.paf[r, rows(xl * 64, 64), :] + v.a1[r].astype(F32)
        v.paf[r, rows(xl * 64, 64), :] = total
        v.sa[r] = total.astype(BF16)
        if r in DIRECT:
            for j in (0, 2, 1):
                send("a2d", r, v.sa.at[r, rows(other_y[j] * 16, 16)], v.a2d.at[r, j], in_row[j])
        else:
            far = rows(y_far * 16, 16)
            send("a2", r, v.sa.at[r, far, pl.ds(0, HA)], v.a2.at[r, 0], above)
            send("a2", r, v.sa.at[r, far, pl.ds(HA, HA)], v.a2.at[r, 1], below)

    def x_sums(r, kind):
        def total(x):
            sums = v.pbf[r, rows(y * 32 + x * 16, 16), :]
            for j in range(3 if kind == "b1d" else 2):
                sums = sums + named[kind][r, j, rows(x * 16, 16), :].astype(F32)
            return sums

        v.sb[r] = total(1 - xl).astype(BF16)
        send("b3", r, v.sb.at[r], v.b3.at[r], x_other)
        v.pbf[r, rows(y * 32 + xl * 16, 16), :] = total(xl)

    def s2b(r):
        if r in DIRECT:
            arrived("b1d", r, v.b1d.at[r])
            x_sums(r, "b1d")
            return
        arrived("b1", r, v.b1.at[r])
        up, down = rows(y_up * 32, 16), rows(y_dn * 32 + 16, 16)
        v.sb2[r, 0, :16] = (v.pbf[r, up, :] + v.b1[r, 0].astype(F32)).astype(BF16)
        v.sb2[r, 0, 16:] = v.pbb[r, rows(y_up * 32 + 16, 16), :]
        send("b2", r, v.sb2.at[r, 0], v.b2.at[r, 0], above)
        v.sb2[r, 1, :16] = v.pbb[r, rows(y_dn * 32, 16), :]
        v.sb2[r, 1, 16:] = (v.pbf[r, down, :] + v.b1[r, 1].astype(F32)).astype(BF16)
        send("b2", r, v.sb2.at[r, 1], v.b2.at[r, 1], below)

    def s3a(r):
        arrived("a2", r, v.a2.at[r])
        up = v.paf[r, rows(xl * 64 + y_up * 16, 16), :]
        v.sa2[r, 0, :, :HA] = (up[:, :HA] + v.a2[r, 0].astype(F32)).astype(BF16)
        v.sa2[r, 0, :, HA:] = up[:, HA:].astype(BF16)
        send("a3", r, v.sa2.at[r, 0], v.a3.at[r, 0], above)
        down = v.paf[r, rows(xl * 64 + y_dn * 16, 16), :]
        v.sa2[r, 1, :, :HA] = down[:, :HA].astype(BF16)
        v.sa2[r, 1, :, HA:] = (down[:, HA:] + v.a2[r, 1].astype(F32)).astype(BF16)
        send("a3", r, v.sa2.at[r, 1], v.a3.at[r, 1], below)

    def s3b(r):
        arrived("b2", r, v.b2.at[r])
        x_sums(r, "b2")

    def s4a(r):
        kind = "a2d" if r in DIRECT else "a3"
        arrived(kind, r, named[kind].at[r])
        mine = rows(xl * 64 + y * 16, 16)
        total = v.paf[r, mine, :]
        for j in range(3 if r in DIRECT else 2):
            total = total + named[kind][r, j].astype(F32)
        v.hid[r, mine, :CA] = jnp.maximum(total + v.ubias[:, :CA], 0.0).astype(BF16)
        here = v.hid.at[r, mine, pl.ds(0, CA)]
        if r in DIRECT:
            for j in (0, 2, 1):
                send("a3d", r, here, here, in_row[j])
        else:
            send("a4", r, here, here, above)
            send("a4", r, here, here, below)

    def s4b(r):
        arrived("b3", r, v.b3.at[r])
        mine = rows(y * 32 + xl * 16, 16)
        total = v.pbf[r, mine, :] + v.b3[r].astype(F32)
        v.hid[r, mine, CA:] = jnp.maximum(total + v.ubias[:, CA:], 0.0).astype(BF16)
        here = v.hid.at[r, mine, pl.ds(CA, CB)]
        send("b4", r, here, here, x_other)

    def s5a(r):
        arrived("a4", r, v.a3.at[r])
        here = v.hid.at[r, rows(xl * 64 + y_dn * 16, 16), pl.ds(0, HA)]
        send("a5", r, here, here, above)
        here = v.hid.at[r, rows(xl * 64 + y_up * 16, 16), pl.ds(HA, HA)]
        send("a5", r, here, here, below)

    def y_back(r):
        arrived("b4", r, v.b3.at[r])
        here = v.hid.at[r, rows(y * 32, 32), pl.ds(CA, CB)]
        if r in DIRECT:
            for j in (0, 2, 1):
                send("b4d", r, here, here, in_row[j])
        else:
            send("b5", r, here, here, above)
            send("b5", r, here, here, below)

    def s5b(r):
        y_back(r)

    def s6a(r):
        if r in DIRECT:
            arrived("a3d", r, v.a2d.at[r])
        else:
            arrived("a5", r, v.a2.at[r])
        here = v.hid.at[r, rows(xl * 64, 64), pl.ds(0, CA)]
        send("a6", r, here, here, x_other)

    def s6b(r):
        if r in DIRECT:
            y_back(r)
            return
        arrived("b5", r, v.b2.at[r])
        here = v.hid.at[r, rows(y_dn * 32, 16), pl.ds(CA, CB)]
        send("b6", r, here, here, above)
        here = v.hid.at[r, rows(y_up * 32 + 16, 16), pl.ds(CA, CB)]
        send("b6", r, here, here, below)

    def g2(r):
        arrived("a6", r, v.a1.at[r])
        if r in DIRECT:
            arrived("b4d", r, v.b1d.at[r])
        else:
            arrived("b6", r, v.b1.at[r])
        for n in range(0, W, 256):
            v.pf[r, :, n:n + 256] = jnp.dot(v.hid[r], v.wdn[:, n:n + 256], preferred_element_type=F32)
        v.so[r] = v.pf[r, rows((1 - c) * 64, 64), :].astype(BF16)
        send("so", r, v.so.at[r], v.sib.at[r], sibling)

    def chip_sum(r, h):
        return v.pf[r, rows(c * 64 + h * PIECE, PIECE), :] + v.sib[r, h * PIECE:(h + 1) * PIECE].astype(F32)

    summed = set()

    def z_sum(r, h):
        if r not in summed:
            arrived("so", r, v.sib.at[r])
            summed.add(r)
        part = pl.ds(h * PIECE, PIECE)
        total = chip_sum(r, h)
        if r in (1, 2, 6, 7) or (r == 3 and h < CUTS // 2) or (r == 5 and h >= CUTS // 2):
            arrived("zr", r * CUTS + h, v.zr.at[r, part])
            total = total + v.zr[r, part].astype(F32)
        v.zs[r, part] = total.astype(BF16)
        step = -1 if r < 4 or (r == 4 and h < CUTS // 2) else 1
        there = (r + step) % N
        there = 4 if there == 0 and step > 0 else there
        send("zr", there * CUTS + h, v.zs.at[r, part], v.zr.at[there, part], ahead if step < 0 else behind)

    def finish(h):
        if 0 not in summed:
            arrived("so", 0, v.sib.at[0])
            summed.add(0)
        part = pl.ds(h * PIECE, PIECE)
        arrived("zr", h, v.zr.at[0, part])
        arrived("zr", 4 * CUTS + h, v.zr.at[4, part])
        mixed = chip_sum(0, h) + v.zr[0, part].astype(F32) + v.zr[4, part].astype(F32)
        out[0, h * PIECE:(h + 1) * PIECE] = (v.xres[h * PIECE:(h + 1) * PIECE] + mixed + v.dbias[...]).astype(BF16)

    first_down = True
    chunk_steps = {
        G1_: g1,
        S2A_: s2a,
        S2B_: s2b,
        S3A_: s3a,
        S3B_: s3b,
        S4A_: s4a,
        S4B_: s4b,
        S5A_: s5a,
        S5B_: s5b,
        S6A_: s6a,
        S6B_: s6b,
        G2_: g2,
    }
    first_up = True
    for name, r, h in ORDER:
        if name == G1_ and first_up:
            loads[5].wait()
            first_up = False
        if name == G2_ and first_down:
            loads[6].wait()
            first_down = False
        if name == GA_:
            ga(r, h)
        elif name == N_:
            normalize(h)
        elif name == Z_ and r == 0:
            finish(h)
        elif name == Z_:
            z_sum(r, h)
        else:
            chunk_steps[name](r)

    sent = dict(
        hand=v.hs, agc=v.zr, agz=v.zr.at[pl.ds(0, 7)], a1=v.a1, a6=v.a1, b3=v.b3, b4=v.b3,
        so=v.sib, zr=v.zr.at[pl.ds(0, 7)],
    )
    by_ring = pl.ds(0, N - len(DIRECT))
    for kind, like in dict(a2="a2", a3="a3", b1="b1", b2="b2", a4="a3", a5="a2", b5="b2", b6="b1").items():
        if len(DIRECT) < N:
            sent[kind] = named[like].at[by_ring]
    for kind, like in dict(a2d="a2d", b1d="b1d", a3d="a2d", b4d="b1d").items():
        if DIRECT:
            sent[kind] = named[like].at[pl.ds(0, len(DIRECT))]
    for kind, like in sent.items():
        pltpu.make_async_copy(like, like, send_sem.at[SENDS.index(kind)]).wait()


def body(handoff, ln_gain, ln_bias, w_up, up_bias, w_down, down_bias):
    return pl.pallas_call(
        kernel,
        out_shape=jax.ShapeDtypeStruct((1, 64, W), BF16),
        in_specs=[pl.BlockSpec(memory_space=pl.ANY)] * 7,
        out_specs=pl.BlockSpec(memory_space=pltpu.VMEM),
        scratch_shapes=[pltpu.VMEM(shape, dtype) for shape, dtype in SCRATCH.values()] + [
            pltpu.SemaphoreType.DMA((7,)),
            pltpu.SemaphoreType.DMA((4,)),
            pltpu.SemaphoreType.DMA((len(SENDS),)),
            pltpu.SemaphoreType.DMA((LANDINGS,)),
        ],
        compiler_params=pltpu.CompilerParams(
            collective_id=0, has_side_effects=True, vmem_limit_bytes=60 << 20
        ),
        name="relay_block",
    )(handoff, ln_gain, ln_bias, w_up, up_bias, w_down, down_bias)


def solution(mesh):
    placed = (
        P("section", ("mp", "dp"), None),
        P("section", "dp"),
        P("section", "dp"),
        P("section", "dp", "mp"),
        P("section", "mp"),
        P("section", "mp", "dp"),
        P("section", "dp"),
    )
    return jax.shard_map(
        body, mesh=mesh, in_specs=placed, out_specs=P("section", "mp", "dp"), check_vma=False
    )
```

time: 82.5 us -> 82.5 us (level)
  no operation moved by 1% of the time
where the time goes in v4:
time: 82.5 us; the launch traced here: 82.4 us
  Pallas kernels  80.8 us (98%)
  local copies, waits for them, and re-layouts  1.62 us (2%)
    pallas_call x1, Pallas kernels, body(): pl.pallas_call(kernel, out_shape=jax.ShapeDtypeStruct((1, 64, W), BF16),...  80.8 us

profile of v4, /device:TPU:4, one launch (start us, length us, event | category | flops | bytes accessed | tf_op | source)
XLA Modules:
  0.0 82.4 jit_solution(6822126351190739773)
XLA Ops:
  0.0 80.8 %relay_block.1 = bf16[1,64,1536]{2,1,0:T(8,128)(2,1)} custom-call(bf16[1,8,12288]{2,1,0:T(8,128)(2,1)} %hand_in.1, f32[1,1536]{1,0:T(1,128)} %gain_in.1, f32[1,1536]{1,0:T(1,128)} %bias_in.1, bf16[1,1536,1536]{2,1,0:T(8,128)(2,1)} %wup_in.1, f32[1,1536]{1,0:T(1,128)} %ubias_in.1, bf16[1,1536,1536]{2,1,0:T(8,128)(2,1)} %wdn_in.1, f32[1,1536]{1,0:T(1,128)} %dbias_in.1), custom_call_target="tpu_custom_call" | custom-call | tf_op jit(solution)/shard_map/relay_block/pallas_call | solution.py:446
  80.8 1.6 %copy.9 = bf16[1,64,1536]{2,1,0:T(8,128)(2,1)} copy(bf16[1,64,1536]{2,1,0:T(8,128)(2,1)} %relay_block.1) | data formatting | bytes 393216
